TPU v7x, 256 devices: a whole 4x4x8 slice. The times are simulated.
256 devices in a mesh: row: 16 (over z, core), col: 16 (over x, y).
Axes of the slice: x: 4, y: 4, z: 8, core: 2. Of those that a mesh axis runs over, the one named last changes fastest.
Arguments:
- right_aquifer: float32 [4, 12, 256, 4096], P(None, None, 'row', 'col'), may hold values from -24 to 24
- right_district: float32 [4, 3072], replicated, may hold values from -24 to 24
- head_scale: float32 [12, 256, 4096], P(None, 'row', 'col'), may hold values from 0.02 to 2
- crop_scale: float32 [6, 256, 4096], P(None, 'row', 'col'), may hold values from 0.02 to 2
- conductance: float32 [2, 256, 4096], P(None, 'row', 'col'), may hold values from 0.1 to 1
- water_use: float32 [12, 6], replicated, may hold values from 0.2 to 1
- climate: float32 [256, 4096], P('row', 'col'), may hold values from 0.5 to 2
- district_use: float32 [6], replicated, may hold values from 0.5 to 1.5
- district_id: int32 [256, 4096], P('row', 'col'), may hold values from 0 to 3071, as said below
- active: int32 [256, 4096], P('row', 'col'), may hold values 0 or 1
Outputs:
- dual_aquifer: float32 [4, 12, 256, 4096], P(None, None, 'row', 'col')
- dual_district: float32 [4, 3072], replicated
- residual_aquifer: float32 [4, 12, 256, 4096], P(None, None, 'row', 'col')
- residual_district: float32 [4, 3072], replicated
Inputs may be any that keep to these rules, and one draw needn't show every extreme that they name: `district_id`: each district's cells form one axis-aligned rectangle of the grid, the districts together cover the grid, and every district has at least one cell.
All inputs are finite; a program needn't handle non-finite values. No bound on the sum of `active` on one device may be relied on, other than what follows from the above.
Results may differ from a plain program's by a relative error of at most 0.0003.
Values sent between devices are 32-bit elements; how exact they have to be, the bound alone decides.
A program may use at most 64 MiB of HBM per device.

v0:
```python
import jax
import jax.numpy as jnp
from jax import lax
from jax.sharding import PartitionSpec as P

ITERS = 4
DHI = 128
DLO = 24


PROXIMAL = 0.05
EXACT = lax.Precision.HIGHEST


def extended(value, sides, width):
    for axis, dim in sides:
        peers, length = (lax.axis_size(axis), value.shape[dim])
        up = [(i, (i + 1) % peers) for i in range(peers - 1)]
        down = [(j, i) for i, j in up]
        last = lax.slice_in_dim(value, length - width, length, axis=dim)
        first = lax.slice_in_dim(value, 0, width, axis=dim)
        before = lax.ppermute(last, axis, up)
        after = lax.ppermute(first, axis, down)
        value = jnp.concatenate([before, value, after], axis=dim)
    return value


def laplace(grid_values, east_faces, south_faces):
    middle = grid_values[..., 1:-1, 1:-1]
    return (
        east_faces[1:-1, 1:-1] * (middle - grid_values[..., 1:-1, 2:])
        + east_faces[1:-1, :-2] * (middle - grid_values[..., 1:-1, :-2])
        + south_faces[1:-1, 1:-1] * (middle - grid_values[..., 2:, 1:-1])
        + south_faces[:-2, 1:-1] * (middle - grid_values[..., :-2, 1:-1])
    )


def body(
    right_aquifer,
    right_district,
    head_scale,
    crop_scale,
    conductance,
    water_use,
    climate,
    district_use,
    district_id,
    active,
):
    rhs_count, months, tile_rows, tile_cols = right_aquifer.shape
    districts = right_district.shape[1]
    cell_count = tile_rows * tile_cols
    grid_cells = tile_rows * lax.axis_size("row") * tile_cols * lax.axis_size("col")
    scale = (districts / grid_cells) ** 0.5
    live = active.astype(jnp.float32)
    weight = live * climate
    coeff = scale * district_use[:, None, None] * live[None]
    flat_ids = district_id.reshape(cell_count)
    hot_high = (lax.iota(jnp.int32, DHI)[:, None] == (flat_ids // DLO)[None, :]).astype(jnp.float32)
    hot_low = (lax.iota(jnp.int32, DLO)[:, None] == (flat_ids % DLO)[None, :]).astype(jnp.float32)

    def to_district(values):
        weighted = values[:, None, :] * hot_low[None]
        summed = jnp.einsum("hn,bln->bhl", hot_high, weighted, precision=EXACT)
        return summed.reshape(values.shape[0], districts)

    def from_district(table_values):
        blocks = table_values.reshape(table_values.shape[0], DHI, DLO)
        picked = jnp.einsum("bhl,hn->bln", blocks, hot_high, precision=EXACT)
        return jnp.sum(picked * hot_low[None], axis=1)

    stacked = jnp.concatenate([conductance, head_scale], axis=0)
    near_stack = extended(stacked, (("row", 1), ("col", 2)), 1)
    east_near = near_stack[0]
    south_near = near_stack[1]
    head_near = near_stack[2:]
    east_here = east_near[1:-1, 1:-1]
    east_west = east_near[1:-1, :-2]
    south_here = south_near[1:-1, 1:-1]
    south_north = south_near[:-2, 1:-1]
    lap_sum = east_here + east_west + south_here + south_north
    diag_aquifer = (
        head_scale * lap_sum * lap_sum
        + east_here * east_here * head_near[:, 1:-1, 2:]
        + east_west * east_west * head_near[:, 1:-1, :-2]
        + south_here * south_here * head_near[:, 2:, 1:-1]
        + south_north * south_north * head_near[:, :-2, 1:-1]
        + weight
        * weight
        * jnp.einsum("mc,cij->mij", water_use * water_use, crop_scale, precision=EXACT)
        + PROXIMAL
    )
    district_local = to_district(
        jnp.sum(coeff * coeff * crop_scale, axis=0).reshape(1, cell_count)
    )[0]
    diag_district = lax.psum(district_local, ("row", "col")) + PROXIMAL

    def head_parts(direc_aq):
        padded = extended(direc_aq, (("row", 2), ("col", 3)), 1)
        grad_head = laplace(padded, east_near, south_near)
        scaled_head = head_scale * grad_head
        padded_scaled = extended(scaled_head, (("row", 2), ("col", 3)), 1)
        head_term = laplace(padded_scaled, east_near, south_near)
        return (grad_head, scaled_head, head_term)

    def product(direc_aq, direc_di):
        grad_head, scaled_head, head_term = head_parts(direc_aq)
        lookup = from_district(direc_di).reshape(rhs_count, tile_rows, tile_cols)
        grad_crop = (
            weight * jnp.einsum("mc,rmij->rcij", water_use, direc_aq, precision=EXACT)
            + coeff[None] * lookup[:, None]
        )
        scaled_crop = crop_scale * grad_crop
        image_aq = (
            head_term
            + weight * jnp.einsum("mc,rcij->rmij", water_use, scaled_crop, precision=EXACT)
            + PROXIMAL * direc_aq
        )
        cell_sum = jnp.sum(coeff[None] * scaled_crop, axis=1).reshape(rhs_count, cell_count)
        partial_rows = to_district(cell_sum)
        energy = (
            jnp.sum(scaled_head * grad_head, axis=(1, 2, 3))
            + jnp.sum(scaled_crop * grad_crop, axis=(1, 2, 3))
            + PROXIMAL * jnp.sum(direc_aq * direc_aq, axis=(1, 2, 3))
        )
        return (image_aq, partial_rows, energy)

    def district_total(partial_rows):
        return lax.psum(partial_rows, ("row", "col"))

    def precond_inner(res_aq, res_di, pre_aq, pre_di):
        local_part = jnp.sum(res_aq * pre_aq, axis=(1, 2, 3))
        return lax.psum(local_part, ("row", "col")) + jnp.sum(res_di * pre_di, axis=1)

    dual_aquifer = jnp.zeros_like(right_aquifer)
    dual_district = jnp.zeros_like(right_district)
    res_aq = right_aquifer
    res_di = right_district
    pre_aq = res_aq / diag_aquifer[None]
    pre_di = res_di / diag_district[None]
    dir_aq = pre_aq
    dir_di = pre_di
    rho = precond_inner(res_aq, res_di, pre_aq, pre_di)
    for repeat in range(ITERS):
        image_aq, partial_rows, energy = product(dir_aq, dir_di)
        image_di = district_total(partial_rows) + PROXIMAL * dir_di
        local_curve = jnp.sum(dir_aq * image_aq, axis=(1, 2, 3))
        curve_total = lax.psum(local_curve, ("row", "col")) + jnp.sum(dir_di * image_di, axis=1)
        alpha = rho / curve_total
        dual_aquifer = dual_aquifer + alpha[:, None, None, None] * dir_aq
        dual_district = dual_district + alpha[:, None] * dir_di
        res_aq = res_aq - alpha[:, None, None, None] * image_aq
        res_di = res_di - alpha[:, None] * image_di
        if repeat + 1 < ITERS:
            pre_aq = res_aq / diag_aquifer[None]
            pre_di = res_di / diag_district[None]
            rho_new = precond_inner(res_aq, res_di, pre_aq, pre_di)
            ratio = rho_new / rho
            dir_aq = pre_aq + ratio[:, None, None, None] * dir_aq
            dir_di = pre_di + ratio[:, None] * dir_di
            rho = rho_new
    image_aq, partial_rows, energy = product(dual_aquifer, dual_district)
    image_di = district_total(partial_rows) + PROXIMAL * dual_district
    return (dual_aquifer, dual_district, right_aquifer - image_aq, right_district - image_di)


def solution(mesh):
    placed = (
        P(None, None, "row", "col"),
        P(),
        P(None, "row", "col"),
        P(None, "row", "col"),
        P(None, "row", "col"),
        P(),
        P("row", "col"),
        P(),
        P("row", "col"),
        P("row", "col"),
    )
    return jax.shard_map(
        body,
        mesh=mesh,
        in_specs=placed,
        out_specs=(P(None, None, "row", "col"), P(), P(None, None, "row", "col"), P()),
        check_vma=False,
    )
```

profile of v0, /device:TPU:1, one launch (start us, length us, event | category | flops | bytes accessed | tf_op | source)
XLA Modules:
  0.0 1047.4 jit_solution(12476204349956083352)
XLA Ops:
  2.5 5.1 collective-permute-start.1
  17.6 79.6 %psum.99 = f32[3072]{0:T(1024)S(1)} all-reduce(f32[3072]{0:T(1024)S(1)} %squeeze_reshape.3), channel_id=1, replica_groups=mesh['row'=16,'col'=16] {'row','col'}, use_global_device_ids=true, to_apply=%region_3.4 | all-reduce | flops 3072 | bytes 24576 | tf_op jit(solution)/shard_map/psum | solution.py:96
  98.6 4.0 collective-permute-start.2
  107.4 4.0 collective-permute-start.5
  118.2 4.9 collective-permute-start.7
  136.2 4.4 collective-permute-start.8
  155.5 4.0 multiply_reduce_fusion.5
  159.5 81.7 %all-reduce.3 = (f32[4]{0:T(128)S(1)}, f32[4,3072]{1,0:T(4,128)S(1)}, f32[4]{0:T(128)S(1)}) all-reduce(f32[4]{0:T(128)} %get-tuple-element.17, f32[4,3072]{1,0:T(4,128)} %reshape.167, f32[4]{0:T(128)} %get-tuple-element.16), channel_id=1, replica_groups=mesh['row'=16,'col'=16] {'row','col'}, use_global_device_ids=true, to_apply=%region_1.2 | all-reduce | flops 12296 | bytes 98368 | tf_op jit(solution)/shard_map/psum | solution.py:133
  243.7 73.7 %psum.102 = f32[4]{0:T(128)S(1)} all-reduce(f32[4]{0:T(128)S(1)} %multiply_reduce_fusion.4), channel_id=1, replica_groups=mesh['row'=16,'col'=16] {'row','col'}, use_global_device_ids=true, to_apply=%region_12.13 | all-reduce | flops 4 | bytes 32 | tf_op jit(solution)/shard_map/psum | solution.py:133
  346.2 4.8 collective-permute-start.16
  374.1 4.6 multiply_reduce_fusion.3
  378.7 80.7 %all-reduce.2 = (f32[4]{0:T(128)S(1)}, f32[4,3072]{1,0:T(4,128)S(1)}) all-reduce(f32[4]{0:T(128)} %get-tuple-element.109, f32[4,3072]{1,0:T(4,128)} %reshape.169), channel_id=1, replica_groups=mesh['row'=16,'col'=16] {'row','col'}, use_global_device_ids=true, to_apply=%region_16.17 | all-reduce | flops 12292 | bytes 98336 | tf_op jit(solution)/shard_map/psum | solution.py:148
  465.9 73.7 %psum.105 = f32[4]{0:T(128)S(1)} all-reduce(f32[4]{0:T(128)} %get-tuple-element.35), channel_id=1, replica_groups=mesh['row'=16,'col'=16] {'row','col'}, use_global_device_ids=true, to_apply=%region_21.22 | all-reduce | flops 4 | bytes 32 | tf_op jit(solution)/shard_map/psum | solution.py:133
  557.5 3.5 collective-permute-start.23
  575.0 4.0 collective-permute-start.24
  602.4 6.8 multiply_reduce_fusion.1
  609.2 80.4 %all-reduce.1 = (f32[4]{0:T(128)}, f32[4,3072]{1,0:T(4,128)}) all-reduce(f32[4]{0:T(128)} %get-tuple-element.113, f32[4,3072]{1,0:T(4,128)} %reshape.171), channel_id=1, replica_groups=mesh['row'=16,'col'=16] {'row','col'}, use_global_device_ids=true, to_apply=%region_25.26 | all-reduce | flops 12292 | bytes 98336 | tf_op jit(solution)/shard_map/psum | solution.py:148
  693.7 74.7 %psum.108 = f32[4]{0:T(128)S(1)} all-reduce(f32[4]{0:T(128)} %multiply_reduce_fusion), channel_id=1, replica_groups=mesh['row'=16,'col'=16] {'row','col'}, use_global_device_ids=true, to_apply=%region_30.31 | all-reduce | flops 4 | bytes 32 | tf_op jit(solution)/shard_map/psum | solution.py:133
  804.4 3.7 collective-permute-start.32
  831.3 5.9 fusion.115
  837.2 80.4 %all-reduce = (f32[4]{0:T(128)}, f32[4,3072]{1,0:T(4,128)}) all-reduce(f32[4]{0:T(128)} %fusion.115, f32[4,3072]{1,0:T(4,128)} %reshape.173), channel_id=1, replica_groups=mesh['row'=16,'col'=16] {'row','col'}, use_global_device_ids=true, to_apply=%region_34.35 | all-reduce | flops 12292 | bytes 98336 | tf_op jit(solution)/shard_map/psum | solution.py:148
  925.0 3.9 collective-permute-start.36
  946.1 4.1 collective-permute-start.40
  952.0 78.5 %psum.111 = f32[4,3072]{1,0:T(4,128)S(1)} all-reduce(f32[4,3072]{1,0:T(4,128)S(1)} %reshape.175), channel_id=1, replica_groups=mesh['row'=16,'col'=16] {'row','col'}, use_global_device_ids=true, to_apply=%region_40.41 | all-reduce | flops 12288 | bytes 98304 | tf_op jit(solution)/shard_map/psum | solution.py:129
  (416 shorter events, 273.5 us)
Async XLA Ops:
  2.5 94.7 %collective-permute-start.1 = (f32[14,1,256]{2,0,1:T(8,128)S(1)}, f32[14,1,256]{2,0,1:T(8,128)S(1)}, u32[]{:S(2)}, u32[]{:S(2)}) collective-permute-start(f32[14,1,256]{2,0,1:T(8,128)S(1)} %get-tuple-element.89), channel_id=1, source_target_pairs={{16,0},{32,16},{48,32},{64,48},{80,64},{96,80},{112,96},{128,112},... | collective-permute-start | bytes 43016 | tf_op jit(solution)/shard_map/ppermute | solution.py:23
  7.6 89.6 %collective-permute-start = (f32[14,1,256]{2,0,1:T(8,128)S(1)}, f32[14,1,256]{2,0,1:T(8,128)S(1)}, u32[]{:S(2)}, u32[]{:S(2)}) collective-permute-start(f32[14,1,256]{2,0,1:T(8,128)S(1)} %get-tuple-element.90), channel_id=1, source_target_pairs={{0,16},{16,32},{32,48},{48,64},{64,80},{80,96},{96,112},{112,128},... | collective-permute-start | bytes 43016 | tf_op jit(solution)/shard_map/ppermute | solution.py:22
  107.4 7.8 collective-permute-start.5
  118.2 11.0 %collective-permute-start.7 = (f32[4,12,18,1]{2,0,3,1:T(4,128)S(1)}, f32[4,12,18,1]{2,0,3,1:T(4,128)}, u32[]{:S(2)}, u32[]{:S(2)}) collective-permute-start(f32[4,12,18,1]{2,0,3,1:T(4,128)S(1)} %copy.69), channel_id=1, source_target_pairs={{0,1},{1,2},{2,3},{3,4},{4,5},{5,6},{6,7},{7,8},{8,9},{9,10},{10,1... | collective-permute-start | bytes 10376 | tf_op jit(solution)/shard_map/ppermute | solution.py:22
  133.2 9.8 collective-permute-start.9
  144.5 9.7 collective-permute-start.11
  331.3 8.9 collective-permute-start.15
  343.7 9.7 collective-permute-start.17
  359.4 12.7 %collective-permute-start.19 = (f32[4,12,18,1]{2,0,3,1:T(4,128)}, f32[4,12,18,1]{2,0,3,1:T(4,128)}, u32[]{:S(2)}, u32[]{:S(2)}) collective-permute-start(f32[4,12,18,1]{2,0,3,1:T(4,128)} %copy.86), channel_id=1, source_target_pairs={{0,1},{1,2},{2,3},{3,4},{4,5},{5,6},{6,7},{7,8},{8,9},{9,10},{10,1... | collective-permute-start | bytes 10376 | tf_op jit(solution)/shard_map/ppermute | solution.py:22
  362.4 7.7 collective-permute-start.18
  542.8 8.4 collective-permute-start.21
  557.5 10.8 %collective-permute-start.23 = (f32[4,12,18,1]{2,0,3,1:T(4,128)}, f32[4,12,18,1]{2,0,3,1:T(4,128)}, u32[]{:S(2)}, u32[]{:S(2)}) collective-permute-start(f32[4,12,18,1]{2,0,3,1:T(4,128)} %copy.92), channel_id=1, source_target_pairs={{0,1},{1,2},{2,3},{3,4},{4,5},{5,6},{6,7},{7,8},{8,9},{9,10},{10,1... | collective-permute-start | bytes 10376 | tf_op jit(solution)/shard_map/ppermute | solution.py:22
  572.5 8.9 collective-permute-start.25
  587.4 12.9 %collective-permute-start.27 = (f32[4,12,18,1]{2,0,3,1:T(4,128)}, f32[4,12,18,1]{2,0,3,1:T(4,128)}, u32[]{:S(2)}, u32[]{:S(2)}) collective-permute-start(f32[4,12,18,1]{2,0,3,1:T(4,128)} %copy.96), channel_id=1, source_target_pairs={{0,1},{1,2},{2,3},{3,4},{4,5},{5,6},{6,7},{7,8},{8,9},{9,10},{10,1... | collective-permute-start | bytes 10376 | tf_op jit(solution)/shard_map/ppermute | solution.py:22
  590.6 7.7 collective-permute-start.26
  772.4 8.2 collective-permute-start.29
  786.9 10.8 %collective-permute-start.31 = (f32[4,12,18,1]{2,0,3,1:T(4,128)}, f32[4,12,18,1]{2,0,3,1:T(4,128)}, u32[]{:S(2)}, u32[]{:S(2)}) collective-permute-start(f32[4,12,18,1]{2,0,3,1:T(4,128)} %copy.102), channel_id=1, source_target_pairs={{0,1},{1,2},{2,3},{3,4},{4,5},{5,6},{6,7},{7,8},{8,9},{9,10},{10,1... | collective-permute-start | bytes 10376 | tf_op jit(solution)/shard_map/ppermute | solution.py:22
  801.9 8.6 collective-permute-start.33
  816.5 12.7 %collective-permute-start.35 = (f32[4,12,18,1]{2,0,3,1:T(4,128)}, f32[4,12,18,1]{2,0,3,1:T(4,128)}, u32[]{:S(2)}, u32[]{:S(2)}) collective-permute-start(f32[4,12,18,1]{2,0,3,1:T(4,128)} %copy.106), channel_id=1, source_target_pairs={{0,1},{1,2},{2,3},{3,4},{4,5},{5,6},{6,7},{7,8},{8,9},{9,10},{10,1... | collective-permute-start | bytes 10376 | tf_op jit(solution)/shard_map/ppermute | solution.py:22
  819.5 7.7 collective-permute-start.34
  922.3 8.9 collective-permute-start.37
  932.4 8.2 collective-permute-start.39
  943.9 86.5 %collective-permute-start.41 = (f32[4,12,1,256]{3,1,2,0:T(8,128)S(1)}, f32[4,12,1,256]{3,1,2,0:T(8,128)S(1)}, u32[]{:S(2)}, u32[]{:S(2)}) collective-permute-start(f32[4,12,1,256]{3,1,2,0:T(8,128)S(1)} %get-tuple-element.65), channel_id=1, source_target_pairs={{16,0},{32,16},{48,32},{64,48},{80,64},{96,80},{112,96},{128,112},... | collective-permute-start | bytes 147464 | tf_op jit(solution)/shard_map/ppermute | solution.py:23
  946.1 84.4 %collective-permute-start.40 = (f32[4,12,1,256]{3,1,2,0:T(8,128)S(1)}, f32[4,12,1,256]{3,1,2,0:T(8,128)S(1)}, u32[]{:S(2)}, u32[]{:S(2)}) collective-permute-start(f32[4,12,1,256]{3,1,2,0:T(8,128)S(1)} %get-tuple-element.66), channel_id=1, source_target_pairs={{0,16},{16,32},{32,48},{48,64},{64,80},{80,96},{96,112},{112,128},... | collective-permute-start | bytes 147464 | tf_op jit(solution)/shard_map/ppermute | solution.py:22
  (103 other events, 1741.2 us)
where the time goes:
time: 1060 us; the launch traced here: 1050 us
  blocking collectives  703 us (66%)
  starting transfers between devices  121 us (11%)
  local copies, waits for them, and re-layouts  104 us (10%)
  matrix products  58.2 us (5%)
  other arithmetic  47.6 us (4%)
  waiting for transfers between devices  11.1 us (1%)
    psum x4, blocking collectives, precond_inner(): lax.psum(local_part, ('row', 'col')) + jnp.sum(res_di * pre_di, axis=1)  304 us
    psum x3, blocking collectives, body(): lax.psum(local_curve, ('row', 'col')) + jnp.sum(dir_di * image_di, axis=1)  241 us
    psum x1, blocking collectives, body(): diag_district = lax.psum(district_local, ('row', 'col')) + PROXIMAL  79.6 us
    psum x1, blocking collectives, district_total(): return lax.psum(partial_rows, ('row', 'col'))  78.5 us
    ppermute x22, starting transfers between devices, extended(): before = lax.ppermute(last, axis, up)  74.2 us
    ppermute x22, starting transfers between devices, extended(): after = lax.ppermute(first, axis, down)  46.6 us
    slice x31, local copies, waits for them, and re-layouts, extended(): first = lax.slice_in_dim(value, 0, width, axis=dim)  25.8 us
    dot_general x5, matrix products, product(): jnp.einsum('mc,rcij->rmij', water_use, scaled_crop, precision=EXACT)  24.5 us
  transfers between devices with their start and end apart: 44, of which 11 were waited for; matrix products, arithmetic and copies ran while one was open for 8% of the time, Pallas kernels for 0%

commit v1 on v0

v1 whole, which is shorter than its diff:
```python
import functools

import jax
import jax.numpy as jnp
from jax import lax
from jax.experimental import pallas as pl
from jax.experimental.pallas import tpu as pltpu
from jax.sharding import PartitionSpec as P

ITERS = 4
RHS = 4
MONTHS = 12
CROPS = 6
FIELDS = RHS * MONTHS
DHI = 8
DLO = 384
LANES = 128
TILE_ROWS = 16
CHUNKS = 32
PROXIMAL = 0.05
SHIFTS = (0.5, 8.0, 3.0, 1.0)
PAIRS = tuple((i, j) for i in range(ITERS) for j in range(i, ITERS))
MESH = pl.DeviceIdType.MESH
F32 = jnp.float32
CORE = pl.ds(8, 16)


def lanes_of(shape):
    return lax.broadcasted_iota(jnp.int32, shape, len(shape) - 1)


def rows_of(shape):
    return lax.broadcasted_iota(jnp.int32, shape, len(shape) - 2)


def beside(tiles):
    axis = tiles[0].ndim - 1
    lane = lanes_of(tiles[0].shape)
    ahead = [pltpu.roll(t, LANES - 1, axis) for t in tiles]
    behind = [pltpu.roll(t, 1, axis) for t in tiles]
    east = [jnp.where(lane == LANES - 1, ahead[(n + 1) % 3], ahead[n]) for n in range(3)]
    west = [jnp.where(lane == 0, behind[(n + 2) % 3], behind[n]) for n in range(3)]
    return east, west


def kernel(
    grid_cells,
    rhs_ref,
    rdi_ref,
    head_ref,
    crop_ref,
    cond_ref,
    climate_ref,
    id_ref,
    active_ref,
    wu_ref,
    use_ref,
    dual_ref,
    dual_di_ref,
    res_ref,
    res_di_ref,
    basis,
    image,
    stat,
    coef,
    headw,
    coefc,
    diag,
    dinv,
    cross,
    crossd,
    wcs,
    inner,
    grads,
    hot,
    lo_id,
    hi_id,
    cells,
    looks,
    segacc,
    table,
    diag_di,
    wide,
    bdi,
    sum_in,
    sum_near,
    sum_z,
    sum_out,
    late_near,
    late_z,
    late_in,
    factors,
    row_out,
    row_in,
    col_out,
    col_in,
    xch_send,
    xch_recv,
    sum_send,
    sum_recv,
):
    rows, cols = lax.axis_size("row"), lax.axis_size("col")
    chips, group = rows // 2, 2 * cols
    per = CHUNKS // group
    row, col = lax.axis_index("row"), lax.axis_index("col")
    chip, core = row // 2, lax.rem(row, 2)
    mine = core * cols + col
    districts = DHI * DLO

    def peer(k):
        other = lax.rem(mine + k, group)
        return other, (chip * 2 + other // cols, lax.rem(other, cols))

    def stack(k):
        return (lax.rem(row + 2 * k, rows), col)

    def around(dr, dc):
        return (lax.rem(row + dr + rows, rows), lax.rem(col + dc + cols, cols))

    barrier = pltpu.get_barrier_semaphore()

    def greet(k, carry):
        pl.semaphore_signal(barrier, inc=1, device_id=peer(k)[1], device_id_type=MESH)
        return carry

    def greet_stack(k, carry):
        pl.semaphore_signal(barrier, inc=1, device_id=stack(k), device_id_type=MESH)
        return carry

    lax.fori_loop(1, group, greet, 0)
    lax.fori_loop(1, chips, greet_stack, 0)
    offsets = [(dr, dc) for dr in (-1, 0, 1) for dc in (-1, 0, 1) if dr or dc]
    for dr, dc in offsets:
        pl.semaphore_signal(barrier, inc=1, device_id=around(dr, dc), device_id_type=MESH)

    north = jnp.where(row > 0, 1.0, 0.0).astype(F32)
    south = jnp.where(row < rows - 1, 1.0, 0.0).astype(F32)
    west = jnp.where(col > 0, 1.0, 0.0).astype(F32)
    east = jnp.where(col < cols - 1, 1.0, 0.0).astype(F32)

    def halo_copies(n, quads, groups):
        ahead, back = pl.ds(8, 8), pl.ds(0, 8)
        plan = [
            (row_out.at[n, 0, pl.ds(0, quads)], row_in.at[n, 0, pl.ds(0, quads)], (1, 0)),
            (row_out.at[n, 1, pl.ds(0, quads)], row_in.at[n, 1, pl.ds(0, quads)], (-1, 0)),
            (col_out.at[n, pl.ds(0, groups)], col_in.at[n, 0, pl.ds(0, groups), CORE], (0, 1)),
            (col_out.at[n, pl.ds(0, groups)], col_in.at[n, 1, pl.ds(0, groups), CORE], (0, -1)),
            (col_out.at[n, pl.ds(0, groups), ahead], col_in.at[n, 0, pl.ds(0, groups), pl.ds(0, 8)], (1, 1)),
            (col_out.at[n, pl.ds(0, groups), ahead], col_in.at[n, 1, pl.ds(0, groups), pl.ds(0, 8)], (1, -1)),
            (col_out.at[n, pl.ds(0, groups), back], col_in.at[n, 0, pl.ds(0, groups), pl.ds(24, 8)], (-1, 1)),
            (col_out.at[n, pl.ds(0, groups), back], col_in.at[n, 1, pl.ds(0, groups), pl.ds(24, 8)], (-1, -1)),
        ]
        return [
            pltpu.make_async_remote_copy(
                src_ref=src,
                dst_ref=dst,
                send_sem=xch_send.at[n, k],
                recv_sem=xch_recv.at[n, k],
                device_id=around(*to),
                device_id_type=MESH,
            )
            for k, (src, dst, to) in enumerate(plan)
        ]

    def halo_pack(n, ref, base, quads):
        lane = lanes_of((TILE_ROWS, LANES))

        def cols_of(f, packed, slot):
            both = jnp.where(lane < 64, ref[base + f, 0, CORE], ref[base + f, 1, CORE])
            moved = pltpu.roll(both, lax.rem(4 * slot + 2, LANES), 1)
            return jnp.where(lane // 4 == slot, moved, packed)

        for g in range((quads + 7) // 8):
            count = min(32, 4 * quads - 32 * g)

            def quad(k, packed):
                for u in range(4):
                    packed = cols_of(32 * g + 4 * k + u, packed, 4 * k + u)
                return packed

            col_out[n, g] = lax.fori_loop(0, count // 4, quad, jnp.zeros((TILE_ROWS, LANES), F32))

        def rows_quad(k, carry):
            for u in range(4):
                field = ref.at[base + 4 * k + u]
                for t in range(2):
                    row_out[n, 0, k, t, pl.ds(2 * u, 2)] = field[t, pl.ds(22, 2)]
                    row_out[n, 1, k, t, pl.ds(2 * u, 2)] = field[t, pl.ds(8, 2)]
            return carry

        lax.fori_loop(0, quads, rows_quad, 0)

    def halo_unpack(n, ref, base, quads):
        shape = (32, LANES)
        lane, place = lanes_of(shape), rows_of(shape)
        side = jnp.where(lax.rem(lane, 4) < 2, west, east)
        side = side * jnp.where(place < 8, north, jnp.where(place >= 24, south, 1.0))
        for g in range((quads + 7) // 8):
            count = min(32, 4 * quads - 32 * g)
            packed = jnp.where(lax.rem(lane, 4) < 2, col_in[n, 0, g], col_in[n, 1, g]) * side

            def quad(k, carry):
                for u in range(4):
                    slot = 4 * k + u
                    moved = pltpu.roll(packed, lax.rem(2 * LANES - 4 * slot - 2, LANES), 1)
                    ref[base + 32 * g + slot, 2] = moved
                return carry

            lax.fori_loop(0, count // 4, quad, 0)

        def rows_quad(k, carry):
            for u in range(4):
                for t in range(2):
                    ref[base + 4 * k + u, t, pl.ds(6, 2)] = row_in[n, 0, k, t, pl.ds(2 * u, 2)] * north
                    ref[base + 4 * k + u, t, pl.ds(24, 2)] = row_in[n, 1, k, t, pl.ds(2 * u, 2)] * south
            return carry

        lax.fori_loop(0, quads, rows_quad, 0)

    def bytes_of(ref, sem):
        pltpu.make_async_copy(ref, ref, sem).wait()

    def sum_scatter(n):
        def scatter(k, carry):
            other, device = peer(k)
            pltpu.make_async_remote_copy(
                src_ref=sum_in.at[n, other],
                dst_ref=sum_near.at[n, k],
                send_sem=sum_send.at[n, 0],
                recv_sem=sum_recv.at[n, 0],
                device_id=device,
                device_id_type=MESH,
            ).start()
            return carry

        lax.fori_loop(1, group, scatter, 0)
        sum_near[n, 0] = sum_in[n, mine]

    def sum_spread(n):
        bytes_of(sum_near.at[n, pl.ds(1, group - 1)], sum_recv.at[n, 0])
        sum_z[n, chip] = jnp.sum(sum_near[n], axis=0)

        def spread(k, carry):
            pltpu.make_async_remote_copy(
                src_ref=sum_z.at[n, chip],
                dst_ref=sum_z.at[n, chip],
                send_sem=sum_send.at[n, 1],
                recv_sem=sum_recv.at[n, 1],
                device_id=stack(k),
                device_id_type=MESH,
            ).start()
            return carry

        lax.fori_loop(1, chips, spread, 0)

    def sum_gather(n):
        bytes_of(sum_z.at[n, pl.ds(1, chips - 1)], sum_recv.at[n, 1])
        sum_out[n, mine] = jnp.sum(sum_z[n], axis=0)

        def gather(k, carry):
            pltpu.make_async_remote_copy(
                src_ref=sum_out.at[n, mine],
                dst_ref=sum_out.at[n, mine],
                send_sem=sum_send.at[n, 2],
                recv_sem=sum_recv.at[n, 2],
                device_id=peer(k)[1],
                device_id_type=MESH,
            ).start()
            return carry

        lax.fori_loop(1, group, gather, 0)

    def sum_done(n):
        bytes_of(sum_near.at[n, pl.ds(1, group - 1)], sum_recv.at[n, 2])

    def sum_drain(n):
        bytes_of(sum_near.at[n, pl.ds(1, group - 1)], sum_send.at[n, 0])
        bytes_of(sum_z.at[n, pl.ds(1, chips - 1)], sum_send.at[n, 1])
        bytes_of(sum_near.at[n, pl.ds(1, group - 1)], sum_send.at[n, 2])

    def chunk(k):
        return k // per, pl.ds(8 * (k % per), 8)

    def to_district(n, count, first):
        segacc[...] = jnp.zeros_like(segacc)
        size = count * DHI

        def line(i, carry):
            value = cells[pl.ds(0, count), pl.ds(i, 1), :]
            high = value.astype(jnp.bfloat16).astype(F32)
            here = (hi_id[pl.ds(i, 1), :] == rows_of((DHI, 2 * LANES)))[None]
            total = jnp.zeros((size, DLO), F32)
            for part in (high, value - high):
                spread = jnp.where(here, jnp.broadcast_to(part, (count, DHI, 2 * LANES)), 0.0)
                total += lax.dot_general(
                    spread.reshape(size, 2 * LANES).astype(jnp.bfloat16),
                    hot[i],
                    (((1,), (1,)), ((), ())),
                    preferred_element_type=F32,
                )
            segacc[pl.ds(0, size), :] += total
            return carry

        lax.fori_loop(0, TILE_ROWS, line, 0)
        for b in range(count):
            for t in range(3):
                at, part = chunk(3 * (first + b) + t)
                sum_in[n, at, part] = segacc[pl.ds(DHI * b, DHI), pl.ds(LANES * t, LANES)]

    def from_district(slot, count, first):
        values = jnp.concatenate(
            [
                jnp.concatenate([table[slot + s, r, t] for t in range(3)], axis=1)
                for s in range(count)
                for r in range(RHS)
            ],
            axis=0,
        )
        high = values.astype(jnp.bfloat16)
        low = (values - high.astype(F32)).astype(jnp.bfloat16)

        def line(i, carry):
            hot_here = hot[i]
            picked = jnp.dot(high, hot_here, preferred_element_type=F32) + jnp.dot(
                low, hot_here, preferred_element_type=F32
            )
            here = (hi_id[pl.ds(i, 1), :] == rows_of((DHI, 2 * LANES)))[None]
            picked = jnp.where(here, picked.reshape(count * RHS, DHI, 2 * LANES), 0.0)
            looks[pl.ds(first, count * RHS), pl.ds(i, 1), :] = jnp.sum(picked, axis=1, keepdims=True)
            return carry

        lax.fori_loop(0, TILE_ROWS, line, 0)

    def cells_of(load, first):
        def one(r, carry):
            for t in range(2):
                total = jnp.zeros((TILE_ROWS, LANES), F32)
                for m in range(MONTHS):
                    total += cross[m, t] * load(r * MONTHS + m, t)
                cells[first + r, :, pl.ds(LANES * t, LANES)] = total
            return carry

        lax.fori_loop(0, RHS, one, 0)

    def core_of(slot):
        return lambda f, t: basis[slot * FIELDS + f, t, CORE]

    def smooth(slot):
        def one(r, carry):
            base = slot * FIELDS + r * MONTHS
            for mb in range(0, MONTHS, 4):
                months = pl.ds(base + mb, 4)
                here = [basis[months, t, pl.ds(4, 24)] for t in range(3)]
                e, w = beside(here)
                for t in range(3):
                    n_val = basis[months, t, pl.ds(3, 24)]
                    s_val = basis[months, t, pl.ds(5, 24)]
                    lap = coef[4, t] * here[t] - coef[0, t] * e[t] - coef[1, t] * w[t]
                    lap = lap - coef[2, t] * s_val - coef[3, t] * n_val
                    inner[pl.ds(mb, 4), t] = headw[pl.ds(mb, 4), t] * lap
            for t in range(2):
                totals = [jnp.zeros((TILE_ROWS, LANES), F32)] * CROPS
                for m in range(MONTHS):
                    value = basis[base + m, t, CORE]
                    totals = [totals[c] + wu_ref[m, c] * value for c in range(CROPS)]
                for c in range(CROPS):
                    grads[c, t] = totals[c] * wcs[c, t]
            for mb in range(0, MONTHS, 4):
                here = [inner[pl.ds(mb, 4), t, pl.ds(4, 16)] for t in range(3)]
                e, w = beside(here)
                for t in range(2):
                    n_val = inner[pl.ds(mb, 4), t, pl.ds(3, 16)]
                    s_val = inner[pl.ds(mb, 4), t, pl.ds(5, 16)]
                    lap = coefc[4, t] * here[t] - coefc[0, t] * e[t] - coefc[1, t] * w[t]
                    lap = lap - coefc[2, t] * s_val - coefc[3, t] * n_val
                    lap = lap + PROXIMAL * basis[pl.ds(base + mb, 4), t, CORE]
                    for u in range(4):
                        m = mb + u
                        total = lap[u]
                        for c in range(CROPS):
                            total = total + wu_ref[m, c] * grads[c, t]
                        image[r * MONTHS + m, t] = dinv[m, t] * total
            return carry

        lax.fori_loop(0, RHS, one, 0)

    def advance(slot, look, shift):
        def one(r, carry):
            for t in range(2):
                seen = looks[look + r, :, pl.ds(LANES * t, LANES)]
                for m in range(MONTHS):
                    f = r * MONTHS + m
                    basis[(slot + 1) * FIELDS + f, t, CORE] = (
                        image[f, t] + crossd[m, t] * seen - shift * basis[slot * FIELDS + f, t, CORE]
                    )
            return carry

        lax.fori_loop(0, RHS, one, 0)

    for t in range(2):
        span = pl.ds(LANES * t, LANES)
        for k in range(2):
            stat[k, t, CORE] = cond_ref[k, :, span]
        for m in range(MONTHS):
            stat[2 + m, t, CORE] = head_ref[m, :, span]
        for k in range(2 + MONTHS, 16):
            stat[k, t, CORE] = jnp.zeros((TILE_ROWS, LANES), F32)
    halo_pack(0, stat, 0, 4)
    pl.semaphore_wait(barrier, group + chips - 2 + len(offsets))
    halo_stat = halo_copies(0, 4, 1)
    for copy in halo_stat:
        copy.start()

    scale = (districts / grid_cells) ** 0.5
    ids = id_ref[...]
    high_id = jnp.zeros_like(ids)
    for k in range(1, DHI):
        high_id = high_id + jnp.where(ids >= k * DLO, 1, 0)
    hi_id[...] = high_id
    lo_id[...] = ids - DLO * high_id

    def hot_line(i, carry):
        same = lo_id[pl.ds(i, 1), :] == rows_of((DLO, 2 * LANES))
        hot[i] = jnp.where(same, 1.0, 0.0).astype(jnp.bfloat16)
        return carry

    lax.fori_loop(0, TILE_ROWS, hot_line, 0)
    for t in range(2):
        span = pl.ds(LANES * t, LANES)
        live = active_ref[:, span].astype(F32)
        weight = live * climate_ref[:, span]
        crops = [crop_ref[c, :, span] for c in range(CROPS)]
        own = jnp.zeros((TILE_ROWS, LANES), F32)
        for c in range(CROPS):
            use = scale * use_ref[c] * live
            own = own + use * use * crops[c]
            wcs[c, t] = weight * weight * crops[c]
        cells[0, :, span] = own
        for m in range(MONTHS):
            square = jnp.zeros((TILE_ROWS, LANES), F32)
            mixed = jnp.zeros((TILE_ROWS, LANES), F32)
            for c in range(CROPS):
                drawn = wu_ref[m, c] * crops[c]
                square = square + wu_ref[m, c] * drawn
                mixed = mixed + use_ref[c] * drawn
            diag[m, t] = weight * weight * square + PROXIMAL
            cross[m, t] = weight * live * (scale * mixed)
    for r in range(RHS):
        for hi in range(DHI):
            for t in range(3):
                at = LANES * (3 * hi + t)
                bdi[r, t, pl.ds(hi, 1)] = rdi_ref[pl.ds(r, 1), pl.ds(at, LANES)]

    for copy in halo_stat:
        copy.wait_recv()
    halo_unpack(0, stat, 0, 4)
    window = pl.ds(4, 24)
    faces = [[stat[k, t, window] for t in range(3)] for k in range(2)]
    east_side, west_side = beside(faces[0])
    for t in range(3):
        south_north = stat[1, t, pl.ds(3, 24)]
        coef[0, t] = faces[0][t]
        coef[1, t] = west_side[t]
        coef[2, t] = faces[1][t]
        coef[3, t] = south_north
        coef[4, t] = faces[0][t] + west_side[t] + faces[1][t] + south_north
    for k in range(5):
        for t in range(2):
            coefc[k, t] = coef[k, t, pl.ds(4, 16)]

    def month_diag(m, carry):
        for t in range(3):
            headw[m, t] = stat[2 + m, t, window]
        here = [stat[2 + m, t, CORE] for t in range(3)]
        e, w = beside(here)
        for t in range(2):
            fe, fw, fs, fn, total = [coefc[k, t] for k in range(5)]
            value = diag[m, t] + here[t] * total * total + fe * fe * e[t] + fw * fw * w[t]
            value = value + fs * fs * stat[2 + m, t, pl.ds(9, 16)] + fn * fn * stat[2 + m, t, pl.ds(7, 16)]
            diag[m, t] = value
            inverse = 1.0 / value
            dinv[m, t] = inverse
            crossd[m, t] = cross[m, t] * inverse
        return carry

    lax.fori_loop(0, MONTHS, month_diag, 0)

    def start_basis(r, carry):
        for t in range(2):
            for m in range(MONTHS):
                f = r * MONTHS + m
                basis[f, t, CORE] = rhs_ref[f, :, pl.ds(LANES * t, LANES)] * dinv[m, t]
        return carry

    lax.fori_loop(0, RHS, start_basis, 0)

    halo_pack(1, basis, 0, FIELDS // 4)
    halo_first = halo_copies(1, FIELDS // 4, 2)
    for copy in halo_first:
        copy.start()
    for t in range(2):
        total = jnp.zeros((TILE_ROWS, LANES), F32)
        for m in range(MONTHS):
            total += cross[m, t] * crossd[m, t]
        cells[1, :, pl.ds(LANES * t, LANES)] = total
    cells_of(core_of(0), 2)
    sum_in[...] = jnp.zeros_like(sum_in)
    to_district(0, 2 + RHS, 0)
    sum_scatter(0)

    for copy in halo_first:
        copy.wait_recv()
    halo_unpack(1, basis, 0, FIELDS // 4)
    sum_spread(0)
    smooth(0)
    cells_of(lambda f, t: image[f, t], 0)
    to_district(1, RHS, 0)
    sum_scatter(1)
    sum_gather(0)
    sum_done(0)

    def total_of(n, b):
        return jnp.stack([sum_out[(n,) + chunk(3 * b + t)] for t in range(3)])

    diag_di[...] = total_of(0, 0) + PROXIMAL
    wide[...] = total_of(0, 1)
    for r in range(RHS):
        t0 = bdi[r] / diag_di[...]
        table[0, r] = t0
        table[1, r] = total_of(0, 2 + r) / diag_di[...] + (1 - SHIFTS[0]) * t0
    from_district(0, 2, 0)
    advance(0, 0, SHIFTS[0])
    halo_pack(2, basis, FIELDS, FIELDS // 4)
    halo_second = halo_copies(2, FIELDS // 4, 2)
    for copy in halo_second:
        copy.start()
    sum_spread(1)
    for copy in halo_second:
        copy.wait_recv()
    halo_unpack(2, basis, FIELDS, FIELDS // 4)
    smooth(1)
    advance(1, RHS, SHIFTS[1])
    halo_pack(3, basis, 2 * FIELDS, FIELDS // 4)
    halo_third = halo_copies(3, FIELDS // 4, 2)
    for copy in halo_third:
        copy.start()
    sum_gather(1)
    cells_of(core_of(2), 0)
    to_district(2, RHS, 0)
    for copy in halo_third:
        copy.wait_recv()
    halo_unpack(3, basis, 2 * FIELDS, FIELDS // 4)
    smooth(2)
    sum_done(1)
    for r in range(RHS):
        z1 = total_of(1, r) + wide[...] * table[0, r] - SHIFTS[0] * total_of(0, 2 + r)
        table[2, r] = z1 / diag_di[...] + (1 - SHIFTS[1]) * table[1, r]
    from_district(2, 1, 0)
    advance(2, 0, SHIFTS[2])
    cells_of(core_of(3), 0)
    to_district(2, RHS, RHS)
    sum_scatter(2)
    halo_pack(4, basis, 3 * FIELDS, FIELDS // 4)
    halo_fourth = halo_copies(4, FIELDS // 4, 2)
    for copy in halo_fourth:
        copy.start()

    shape = (8, LANES)

    def inner_products(r, packed):
        totals = [jnp.zeros(shape, F32) for _ in PAIRS]
        for m in range(MONTHS):
            for t in range(2):
                values = [basis[s * FIELDS + r * MONTHS + m, t, CORE] for s in range(ITERS)]
                scaled = [diag[m, t] * v for v in values]
                for n, (i, j) in enumerate(PAIRS):
                    term = scaled[i] * values[j]
                    totals[n] = totals[n] + (term[:8] + term[8:])
        for n, total in enumerate(totals):
            here = (rows_of(shape) == r) & (lanes_of(shape) == n)
            packed = jnp.where(here, jnp.sum(total, keepdims=True), packed)
        return packed

    packed = lax.fori_loop(0, RHS, inner_products, jnp.zeros(shape, F32))
    for copy in halo_fourth:
        copy.wait_recv()
    halo_unpack(4, basis, 3 * FIELDS, FIELDS // 4)
    sum_spread(2)
    smooth(3)

    def top_product(r, packed):
        total = jnp.zeros(shape, F32)
        for m in range(MONTHS):
            for t in range(2):
                f = r * MONTHS + m
                term = diag[m, t] * basis[3 * FIELDS + f, t, CORE] * image[f, t]
                total = total + (term[:8] + term[8:])
        here = (rows_of(shape) == r) & (lanes_of(shape) == len(PAIRS))
        return jnp.where(here, jnp.sum(total, keepdims=True), packed)

    late_in[...] = lax.fori_loop(0, RHS, top_product, packed)

    def late_first(k, carry):
        pltpu.make_async_remote_copy(
            src_ref=late_in,
            dst_ref=late_near.at[mine],
            send_sem=sum_send.at[3, 0],
            recv_sem=sum_recv.at[3, 0],
            device_id=peer(k)[1],
            device_id_type=MESH,
        ).start()
        return carry

    lax.fori_loop(1, group, late_first, 0)
    late_near[mine] = late_in[...]
    sum_gather(2)
    bytes_of(late_near.at[pl.ds(1, group - 1)], sum_recv.at[3, 0])
    late_z[chip] = jnp.sum(late_near[...], axis=0)

    def late_second(k, carry):
        pltpu.make_async_remote_copy(
            src_ref=late_z.at[chip],
            dst_ref=late_z.at[chip],
            send_sem=sum_send.at[3, 1],
            recv_sem=sum_recv.at[3, 1],
            device_id=stack(k),
            device_id_type=MESH,
        ).start()
        return carry

    lax.fori_loop(1, chips, late_second, 0)
    sum_done(2)
    for r in range(RHS):
        table[3, r] = total_of(2, r) / diag_di[...] + (1 - SHIFTS[2]) * table[2, r]
        table[4, r] = total_of(2, RHS + r) / diag_di[...] + (1 - SHIFTS[3]) * table[3, r]
    from_district(3, 1, 0)

    def district_part(i, j):
        out = jnp.zeros(shape, F32)
        for r in range(RHS):
            if j < ITERS:
                term = diag_di[...] * table[i, r] * table[j, r]
            else:
                term = table[3, r] * (2 * total_of(2, RHS + r) + diag_di[...] * table[3, r])
            line = jnp.sum(jnp.sum(term, axis=0), axis=0, keepdims=True)
            out = jnp.where(rows_of(shape) == r, line, out)
        return out

    parts = [district_part(i, j) for i, j in PAIRS + ((3, ITERS),)]
    bytes_of(late_z.at[pl.ds(1, chips - 1)], sum_recv.at[3, 1])
    totals = jnp.sum(late_z[...], axis=0)
    gram = [[None] * (ITERS + 1) for _ in range(ITERS + 1)]
    values = []
    for n, part in enumerate(parts):
        both = part + jnp.where(lanes_of(shape) == n, totals, 0.0)
        values.append(jnp.broadcast_to(jnp.sum(both, axis=1, keepdims=True), shape))
    for n, (i, j) in enumerate(PAIRS):
        gram[i][j] = gram[j][i] = values[n]
    for i in range(ITERS):
        ahead = values[-1] if i == ITERS - 1 else gram[i + 1][ITERS - 1] + SHIFTS[i] * gram[i][ITERS - 1]
        gram[i][ITERS] = ahead - SHIFTS[ITERS - 1] * gram[i][ITERS - 1]

    one, zero = jnp.ones(shape, F32), jnp.zeros(shape, F32)
    x, res, dirn = [zero] * ITERS, [one] + [zero] * ITERS, [one] + [zero] * (ITERS - 1)
    rho = gram[0][0]
    for it in range(ITERS):
        moved = [zero] * (ITERS + 1)
        for k in range(it + 1):
            moved[k + 1] = moved[k + 1] + dirn[k]
            moved[k] = moved[k] + SHIFTS[k] * dirn[k]
        curve = zero
        for i in range(it + 1):
            line = zero
            for j in range(it + 2):
                line = line + moved[j] * gram[i][j]
            curve = curve + dirn[i] * line
        alpha = rho / curve
        x = [x[i] + alpha * dirn[i] for i in range(ITERS)]
        res = [res[i] - alpha * moved[i] for i in range(ITERS + 1)]
        if it + 1 < ITERS:
            rho_new = zero
            for i in range(it + 2):
                line = zero
                for j in range(it + 2):
                    line = line + res[j] * gram[i][j]
                rho_new = rho_new + res[i] * line
            ratio = rho_new / rho
            rho = rho_new
            dirn = [res[i] + ratio * dirn[i] for i in range(ITERS)]
    for k, value in enumerate(x + res):
        factors[k] = value

    def finish(r, carry):
        xs = [factors[k, pl.ds(r, 1)] for k in range(ITERS)]
        rs = [factors[ITERS + k, pl.ds(r, 1)] for k in range(ITERS + 1)]
        for t in range(2):
            span = pl.ds(LANES * t, LANES)
            seen = looks[r, :, span]
            for m in range(MONTHS):
                f = r * MONTHS + m
                vs = [basis[s * FIELDS + f, t, CORE] for s in range(ITERS)]
                vs.append(image[f, t] + crossd[m, t] * seen - SHIFTS[3] * vs[3])
                dual_ref[f, :, span] = xs[0] * vs[0] + xs[1] * vs[1] + xs[2] * vs[2] + xs[3] * vs[3]
                total = rs[0] * vs[0]
                for k in range(1, ITERS + 1):
                    total = total + rs[k] * vs[k]
                res_ref[f, :, span] = diag[m, t] * total
        return carry

    lax.fori_loop(0, RHS, finish, 0)
    for r in range(RHS):
        xs = [factors[k, pl.ds(r, 1)] for k in range(ITERS)]
        rs = [factors[ITERS + k, pl.ds(r, 1)] for k in range(ITERS + 1)]
        for t in range(3):
            dual = xs[0] * table[0, r, t]
            total = rs[0] * table[0, r, t]
            for k in range(1, ITERS):
                dual = dual + xs[k] * table[k, r, t]
            for k in range(1, ITERS + 1):
                total = total + rs[k] * table[k, r, t]
            total = total * diag_di[t]
            for hi in range(DHI):
                span = pl.ds(LANES * (3 * hi + t), LANES)
                dual_di_ref[pl.ds(r, 1), span] = dual[hi : hi + 1]
                res_di_ref[pl.ds(r, 1), span] = total[hi : hi + 1]

    for copies in (halo_stat, halo_first, halo_second, halo_third, halo_fourth):
        for copy in copies:
            copy.wait_send()
    for n in range(3):
        sum_drain(n)
    bytes_of(late_near.at[pl.ds(1, group - 1)], sum_send.at[3, 0])
    bytes_of(late_z.at[pl.ds(1, chips - 1)], sum_send.at[3, 1])


def body(
    right_aquifer,
    right_district,
    head_scale,
    crop_scale,
    conductance,
    water_use,
    climate,
    district_use,
    district_id,
    active,
):
    rows, cols = lax.axis_size("row"), lax.axis_size("col")
    group, chips = 2 * cols, rows // 2
    per = CHUNKS // group
    tile_rows, tile_cols = climate.shape
    grid_cells = tile_rows * rows * tile_cols * cols
    whole = pl.BlockSpec(memory_space=pltpu.VMEM)
    scalars = pl.BlockSpec(memory_space=pltpu.SMEM)
    block = (FIELDS, tile_rows, tile_cols)
    vmem = lambda *shape: pltpu.VMEM(shape, F32)
    core = (2, TILE_ROWS, LANES)
    outs = pl.pallas_call(
        functools.partial(kernel, grid_cells),
        out_shape=(
            jax.ShapeDtypeStruct(block, F32),
            jax.ShapeDtypeStruct(right_district.shape, F32),
            jax.ShapeDtypeStruct(block, F32),
            jax.ShapeDtypeStruct(right_district.shape, F32),
        ),
        in_specs=[whole] * 8 + [scalars] * 2,
        out_specs=(whole,) * 4,
        scratch_shapes=[
            vmem(ITERS * FIELDS, 3, 32, LANES),
            vmem(FIELDS, *core),
            vmem(16, 3, 32, LANES),
            vmem(5, 3, 24, LANES),
            vmem(MONTHS, 3, 24, LANES),
            vmem(5, *core),
            vmem(MONTHS, *core),
            vmem(MONTHS, *core),
            vmem(MONTHS, *core),
            vmem(MONTHS, *core),
            vmem(CROPS, *core),
            vmem(MONTHS, 3, 24, LANES),
            vmem(CROPS, *core),
            pltpu.VMEM((TILE_ROWS, DLO, 2 * LANES), jnp.bfloat16),
            pltpu.VMEM((TILE_ROWS, 2 * LANES), jnp.int32),
            pltpu.VMEM((TILE_ROWS, 2 * LANES), jnp.int32),
            vmem(2 + RHS, TILE_ROWS, 2 * LANES),
            vmem(2 * RHS, TILE_ROWS, 2 * LANES),
            vmem((2 + RHS) * DHI, DLO),
            vmem(ITERS + 1, RHS, 3, DHI, LANES),
            vmem(3, DHI, LANES),
            vmem(3, DHI, LANES),
            vmem(RHS, 3, DHI, LANES),
            vmem(3, group, 8 * per, LANES),
            vmem(3, group, 8 * per, LANES),
            vmem(3, chips, 8 * per, LANES),
            vmem(3, group, 8 * per, LANES),
            vmem(group, 8, LANES),
            vmem(chips, 8, LANES),
            vmem(8, LANES),
            vmem(2 * ITERS + 1, 8, LANES),
            vmem(5, 2, FIELDS // 4, 2, 8, LANES),
            vmem(5, 2, FIELDS // 4, 2, 8, LANES),
            vmem(5, 2, TILE_ROWS, LANES),
            vmem(5, 2, 2, 32, LANES),
            pltpu.SemaphoreType.DMA((5, 8)),
            pltpu.SemaphoreType.DMA((5, 8)),
            pltpu.SemaphoreType.DMA((4, 3)),
            pltpu.SemaphoreType.DMA((4, 3)),
        ],
        compiler_params=pltpu.CompilerParams(
            collective_id=0, has_side_effects=True, vmem_limit_bytes=48 * 1024 * 1024
        ),
    )(
        right_aquifer.reshape(block),
        right_district,
        head_scale,
        crop_scale,
        conductance,
        climate,
        district_id,
        active,
        water_use,
        district_use,
    )
    dual, dual_di, res, res_di = outs
    return dual.reshape(right_aquifer.shape), dual_di, res.reshape(right_aquifer.shape), res_di


def solution(mesh):
    placed = (
        P(None, None, "row", "col"),
        P(),
        P(None, "row", "col"),
        P(None, "row", "col"),
        P(None, "row", "col"),
        P(),
        P("row", "col"),
        P(),
        P("row", "col"),
        P("row", "col"),
    )
    return jax.shard_map(
        body,
        mesh=mesh,
        in_specs=placed,
        out_specs=(P(None, None, "row", "col"), P(), P(None, None, "row", "col"), P()),
        check_vma=False,
    )
```

time: 1060 us -> 110 us (0.10); the launches traced: 1050 us -> 110 us
  blocking collectives: 703 us -> 0 us
  starting transfers between devices: 121 us -> 0 us
  Pallas kernels: 0 us -> 98.7 us
  local copies, waits for them, and re-layouts: 104 us -> 10.4 us
  matrix products: 58.2 us -> 0 us
  other arithmetic: 47.6 us -> 0 us
  waiting for transfers between devices: 11.1 us -> 0 us
    psum x9 -> x0, blocking collectives: 703 us -> none  [the longest x4 304 us: precond_inner(): lax.psum(local_part, ('row', 'col')) + jnp.sum(res_di * pre_di, axis=1)]
    ppermute x44 -> x0, starting transfers between devices: 121 us -> none  [the longest x22 74.2 us: extended(): before = lax.ppermute(last, axis, up)]
    pallas_call x0 -> x1, Pallas kernels: none -> 98.7 us  [body(): pl.pallas_call(functools.partial(kernel, grid_cells), out_shape=(jax.Shap...]
    dot_general x22 -> x0, matrix products: 58.2 us -> none  [the longest x5 24.5 us: product(): jnp.einsum('mc,rcij->rmij', water_use, scaled_crop, precision=EXACT)]
    slice x41 -> x0, local copies, waits for them, and re-layouts: 38.7 us -> none  [the longest x31 25.8 us: extended(): first = lax.slice_in_dim(value, 0, width, axis=dim)]
    ppermute x20 -> x0, local copies, waits for them, and re-layouts: 33.3 us -> none  [the longest x10 17.4 us: extended(): before = lax.ppermute(last, axis, up)]
    mul x8 -> x0, other arithmetic: 13.8 us -> none  [the longest x5 10.2 us: head_parts(): scaled_head = head_scale * grad_head]
    reduce_sum x10 -> x0, other arithmetic: 12.6 us -> none  [the longest x3 5.6 us: precond_inner(): local_part = jnp.sum(res_aq * pre_aq, axis=(1, 2, 3))]
  transfers between devices with their start and end apart: 44 -> 0, of which waited for: 11 -> 0; matrix products, arithmetic and copies ran while one was open for 8% -> 0% of each run, Pallas kernels for 0% -> 0%
where the time goes in v1:
time: 110 us
  Pallas kernels  98.7 us (90%)
  local copies, waits for them, and re-layouts  10.4 us (9%)
    pallas_call x1, Pallas kernels, body(): pl.pallas_call(functools.partial(kernel, grid_cells), out_shape=(jax.Shap...  98.7 us
    unnamed x23, local copies, waits for them, and re-layouts  10.4 us

profile of v1, /device:TPU:1, one launch (start us, length us, event | category | flops | bytes accessed | tf_op | source)
XLA Modules:
  0.0 109.8 jit_solution(9510272955565780596)
XLA Ops:
  0.6 0.0 copy-start.8
  0.6 0.8 copy.14.wu_ref
  1.4 0.0 copy-done.8
  1.4 0.0 copy-start
  1.4 1.1 %copy-done = f32[4,12,16,256]{3,2,1,0:T(8,128)S(1)} copy-done((f32[4,12,16,256]{3,2,1,0:T(8,128)S(1)}, f32[4,12,16,256]{3,2,1,0:T(8,128)}, u32[]{:S(2)}) %copy-start) | copy-done | bytes 786456
  2.6 0.0 copy-start.1
  2.6 0.9 copy-done.1
  3.5 0.0 copy-start.2
  3.5 0.9 copy-done.2
  4.4 0.0 copy-start.3
  4.4 0.8 copy-done.3
  5.2 0.0 copy-start.4
  5.2 0.8 copy-done.4
  5.9 0.0 copy-start.5
  5.9 0.7 copy-done.5
  6.7 0.0 copy-start.6
  6.7 0.7 copy-done.6
  7.4 0.0 copy-start.7
  7.4 0.7 copy-done.7
  8.1 98.7 %shard_map.129 = (f32[48,16,256]{2,1,0:T(8,128)S(1)}, f32[4,3072]{1,0:T(4,128)S(1)}, f32[48,16,256]{2,1,0:T(8,128)S(1)}, f32[4,3072]{1,0:T(4,128)S(1)}) custom-call(f32[48,16,256]{2,1,0:T(8,128)S(1)} %bitcast.3, f32[4,3072]{1,0:T(4,128)S(1)} %copy-done.3, f32[12,16,256]{2,1,0:T(8,128)S(1)} %copy-done.1, f32[6,16,256]{2,1,0:T(8,128)S(1)} %copy-done.2, ...), custom_call_target="tpu_custom_call" | custom-call | tf_op jit(solution)/shard_map/pallas_call | solution.py:758
  106.8 0.9 copy.19
  107.7 0.6 copy.20
  108.3 0.9 copy.21
  109.2 0.6 copy.22
Async XLA Ops:
  0.6 0.8 copy-start.8
  1.4 1.1 %copy-start = (f32[4,12,16,256]{3,2,1,0:T(8,128)S(1)}, f32[4,12,16,256]{3,2,1,0:T(8,128)}, u32[]{:S(2)}) copy-start(f32[4,12,16,256]{3,2,1,0:T(8,128)} %param.10) | copy-start | bytes 2359300
  2.6 0.9 copy-start.1
  3.5 0.9 copy-start.2
  4.4 0.8 copy-start.3
  5.2 0.8 copy-start.4
  5.9 0.7 copy-start.5
  6.7 0.7 copy-start.6
  7.4 0.7 copy-start.7

commit v2 on v1

--- a/solution.py
+++ b/solution.py
@@ -12,11 +12,13 @@
 MONTHS = 12
 CROPS = 6
 FIELDS = RHS * MONTHS
-DHI = 8
-DLO = 384
+DHI = 16
+DLO = 256
 LANES = 128
 TILE_ROWS = 16
 CHUNKS = 32
+LINES = 21
+ID_FIELD = 14
 PROXIMAL = 0.05
 SHIFTS = (0.5, 8.0, 3.0, 1.0)
 PAIRS = tuple((i, j) for i in range(ITERS) for j in range(i, ITERS))
@@ -45,16 +47,16 @@
 
 def kernel(
     grid_cells,
-    rhs_ref,
-    rdi_ref,
-    head_ref,
-    crop_ref,
-    cond_ref,
-    climate_ref,
-    id_ref,
-    active_ref,
-    wu_ref,
-    use_ref,
+    rhs_hbm,
+    rdi_hbm,
+    head_hbm,
+    crop_hbm,
+    cond_hbm,
+    climate_hbm,
+    id_hbm,
+    active_hbm,
+    wu_hbm,
+    use_hbm,
     dual_ref,
     dual_di_ref,
     res_ref,
@@ -68,7 +70,6 @@
     diag,
     dinv,
     cross,
-    crossd,
     wcs,
     inner,
     grads,
@@ -77,7 +78,13 @@
     hi_id,
     cells,
     looks,
-    segacc,
+    wide_look,
+    spread,
+    rdi_ref,
+    crop_ref,
+    climate_ref,
+    id_ref,
+    active_ref,
     table,
     diag_di,
     wide,
@@ -98,6 +105,9 @@
     xch_recv,
     sum_send,
     sum_recv,
+    load_sem,
+    wu_ref,
+    use_ref,
 ):
     rows, cols = lax.axis_size("row"), lax.axis_size("col")
     chips, group = rows // 2, 2 * cols
@@ -105,7 +115,11 @@
     row, col = lax.axis_index("row"), lax.axis_index("col")
     chip, core = row // 2, lax.rem(row, 2)
     mine = core * cols + col
-    districts = DHI * DLO
+    districts = rdi_ref.shape[1]
+
+    def slot_at(slot):
+        return slot * FIELDS + (MONTHS if slot else 0)
+
 
     def peer(k):
         other = lax.rem(mine + k, group)
@@ -116,6 +130,19 @@
 
     def around(dr, dc):
         return (lax.rem(row + dr + rows, rows), lax.rem(col + dc + cols, cols))
+
+    loads = []
+    for t in range(2):
+        span = pl.ds(LANES * t, LANES)
+        loads.append((cond_hbm.at[:, :, span], stat.at[pl.ds(0, 2), t, CORE]))
+        loads.append((head_hbm.at[:, :, span], stat.at[pl.ds(2, MONTHS), t, CORE]))
+    loads += [(id_hbm, id_ref), (climate_hbm, climate_ref), (active_hbm, active_ref)]
+    loads += [(wu_hbm, wu_ref), (use_hbm, use_ref), (crop_hbm, crop_ref), (rdi_hbm, rdi_ref)]
+    for t in range(2):
+        loads.append((rhs_hbm.at[:, :, pl.ds(LANES * t, LANES)], basis.at[pl.ds(0, FIELDS), t, CORE]))
+    loads = [pltpu.make_async_copy(src, dst, load_sem.at[k]) for k, (src, dst) in enumerate(loads)]
+    for load in loads:
+        load.start()
 
     barrier = pltpu.get_barrier_semaphore()
 
@@ -281,55 +308,54 @@
     def chunk(k):
         return k // per, pl.ds(8 * (k % per), 8)
 
+    def line_span(i):
+        return pl.ds(pl.multiple_of(i * (2 * LANES), 2 * LANES), 2 * LANES)
+
     def to_district(n, count, first):
-        segacc[...] = jnp.zeros_like(segacc)
         size = count * DHI
 
         def line(i, carry):
             value = cells[pl.ds(0, count), pl.ds(i, 1), :]
             high = value.astype(jnp.bfloat16).astype(F32)
             here = (hi_id[pl.ds(i, 1), :] == rows_of((DHI, 2 * LANES)))[None]
-            total = jnp.zeros((size, DLO), F32)
-            for part in (high, value - high):
-                spread = jnp.where(here, jnp.broadcast_to(part, (count, DHI, 2 * LANES)), 0.0)
-                total += lax.dot_general(
-                    spread.reshape(size, 2 * LANES).astype(jnp.bfloat16),
-                    hot[i],
-                    (((1,), (1,)), ((), ())),
-                    preferred_element_type=F32,
-                )
-            segacc[pl.ds(0, size), :] += total
-            return carry
-
-        lax.fori_loop(0, TILE_ROWS, line, 0)
+            for k, part in enumerate((high, value - high)):
+                part = jnp.where(here, jnp.broadcast_to(part, (count, DHI, 2 * LANES)), 0.0)
+                spread[pl.ds(k * size, size), line_span(i)] = part.reshape(size, 2 * LANES).astype(jnp.bfloat16)
+            return carry
+
+        lax.fori_loop(0, TILE_ROWS, line, 0, unroll=2)
+        total = lax.dot_general(
+            hot[:, pl.ds(0, TILE_ROWS * 2 * LANES)], spread[pl.ds(0, 2 * size), :], (((1,), (1,)), ((), ())), preferred_element_type=F32
+        ).T
+        total = total[:size] + total[size:]
         for b in range(count):
-            for t in range(3):
-                at, part = chunk(3 * (first + b) + t)
-                sum_in[n, at, part] = segacc[pl.ds(DHI * b, DHI), pl.ds(LANES * t, LANES)]
-
-    def from_district(slot, count, first):
+            for t in range(2):
+                for h in range(2):
+                    at, part = chunk(4 * (first + b) + 2 * t + h)
+                    sum_in[n, at, part] = total[DHI * b + 8 * h : DHI * b + 8 * h + 8, LANES * t : LANES * (t + 1)]
+
+    def from_district(slot, count, first, lines=TILE_ROWS):
+        size = count * RHS * DHI
         values = jnp.concatenate(
             [
-                jnp.concatenate([table[slot + s, r, t] for t in range(3)], axis=1)
+                jnp.concatenate([table[slot + s, r, t] for t in range(2)], axis=1)
                 for s in range(count)
                 for r in range(RHS)
             ],
             axis=0,
         )
-        high = values.astype(jnp.bfloat16)
-        low = (values - high.astype(F32)).astype(jnp.bfloat16)
+        high = values.astype(jnp.bfloat16).astype(F32)
+        both = jnp.concatenate([high, values - high], axis=0).astype(jnp.bfloat16)
 
         def line(i, carry):
-            hot_here = hot[i]
-            picked = jnp.dot(high, hot_here, preferred_element_type=F32) + jnp.dot(
-                low, hot_here, preferred_element_type=F32
-            )
+            picked = jnp.dot(both, hot[:, line_span(i)], preferred_element_type=F32)
+            picked = (picked[:size] + picked[size:]).reshape(count * RHS, DHI, 2 * LANES)
             here = (hi_id[pl.ds(i, 1), :] == rows_of((DHI, 2 * LANES)))[None]
-            picked = jnp.where(here, picked.reshape(count * RHS, DHI, 2 * LANES), 0.0)
+            picked = jnp.where(here, picked, 0.0)
             looks[pl.ds(first, count * RHS), pl.ds(i, 1), :] = jnp.sum(picked, axis=1, keepdims=True)
             return carry
 
-        lax.fori_loop(0, TILE_ROWS, line, 0)
+        lax.fori_loop(0, lines, line, 0, unroll=3 if lines % 3 == 0 else 2)
 
     def cells_of(load, first):
         def one(r, carry):
@@ -343,11 +369,11 @@
         lax.fori_loop(0, RHS, one, 0)
 
     def core_of(slot):
-        return lambda f, t: basis[slot * FIELDS + f, t, CORE]
-
-    def smooth(slot):
+        return lambda f, t: basis[slot_at(slot) + f, t, CORE]
+
+    def smooth(slot, put):
         def one(r, carry):
-            base = slot * FIELDS + r * MONTHS
+            base = slot_at(slot) + r * MONTHS
             for mb in range(0, MONTHS, 4):
                 months = pl.ds(base + mb, 4)
                 here = [basis[months, t, pl.ds(4, 24)] for t in range(3)]
@@ -362,7 +388,7 @@
                 totals = [jnp.zeros((TILE_ROWS, LANES), F32)] * CROPS
                 for m in range(MONTHS):
                     value = basis[base + m, t, CORE]
-                    totals = [totals[c] + wu_ref[m, c] * value for c in range(CROPS)]
+                    totals = [totals[c] + wu_ref[c, m] * value for c in range(CROPS)]
                 for c in range(CROPS):
                     grads[c, t] = totals[c] * wcs[c, t]
             for mb in range(0, MONTHS, 4):
@@ -378,50 +404,101 @@
                         m = mb + u
                         total = lap[u]
                         for c in range(CROPS):
-                            total = total + wu_ref[m, c] * grads[c, t]
-                        image[r * MONTHS + m, t] = dinv[m, t] * total
+                            total = total + wu_ref[c, m] * grads[c, t]
+                        put(r * MONTHS + m, t, dinv[m, t] * total)
             return carry
 
         lax.fori_loop(0, RHS, one, 0)
+
+    def to_image(f, t, value):
+        image[f, t] = value
+
+    def to_second(f, t, value):
+        basis[slot_at(1) + f, t, CORE] = value
+
+    def advance_wide(shift):
+        window = pl.ds(4, 24)
+
+        def one(r, carry):
+            for t in range(3):
+                seen = wide_look[r, t, window]
+                for m in range(MONTHS):
+                    f = r * MONTHS + m
+                    basis[slot_at(1) + f, t, window] = (
+                        basis[slot_at(1) + f, t, window]
+                        + basis[FIELDS + m, t, window] * seen
+                        - shift * basis[f, t, window]
+                    )
+            return carry
+
+        lax.fori_loop(0, RHS, one, 0)
+
+    def repeat(packed):
+        for width in (4, 8, 16, 32, 64):
+            packed = packed + pltpu.roll(packed, width, 1)
+        return packed
+
+    def fill_wide_look():
+        shape = (24, LANES)
+        own = lanes_of(shape) // 4 == rows_of(shape)
+        for r in range(RHS):
+            for t in range(2):
+                span = pl.ds(LANES * t, LANES)
+                wide_look[r, t, CORE] = looks[r, pl.ds(0, TILE_ROWS), span]
+                wide_look[r, t, pl.ds(6, 2)] = looks[r, pl.ds(16, 2), span]
+                wide_look[r, t, pl.ds(24, 2)] = looks[r, pl.ds(18, 2), span]
+            edge = repeat(jnp.where(own, looks[r, pl.ds(20, 1), pl.ds(0, LANES)], 0.0))
+            wide_look[r, 2, pl.ds(4, 24)] = pltpu.roll(edge, LANES - 2, 1)
+
+    def wide_ids():
+        shape = (24, LANES)
+        edge = pltpu.roll(stat[ID_FIELD, 2, pl.ds(4, 24)], 2, 1)
+        edge = repeat(jnp.where(lanes_of(shape) < 4, edge, 0.0))
+        edge = jnp.sum(jnp.where(lanes_of(shape) // 4 == rows_of(shape), edge, 0.0), axis=0, keepdims=True)
+        lines = [jnp.concatenate([stat[ID_FIELD, t, pl.ds(i, 1)] for t in range(2)], axis=1) for i in (6, 7, 24, 25)]
+        lines.append(jnp.concatenate([edge, edge], axis=1))
+        for k, one in enumerate(lines):
+            ids = one.astype(jnp.int32)
+            hi_id[pl.ds(16 + k, 1), :] = ids // DLO
+            lo_id[pl.ds(16 + k, 1), :] = lax.rem(ids, DLO)
+        lax.fori_loop(TILE_ROWS, LINES, hot_line, 0)
 
     def advance(slot, look, shift):
         def one(r, carry):
             for t in range(2):
-                seen = looks[look + r, :, pl.ds(LANES * t, LANES)]
+                seen = looks[look + r, pl.ds(0, TILE_ROWS), pl.ds(LANES * t, LANES)]
                 for m in range(MONTHS):
                     f = r * MONTHS + m
-                    basis[(slot + 1) * FIELDS + f, t, CORE] = (
-                        image[f, t] + crossd[m, t] * seen - shift * basis[slot * FIELDS + f, t, CORE]
+                    basis[slot_at(slot + 1) + f, t, CORE] = (
+                        image[f, t] + basis[FIELDS + m, t, CORE] * seen - shift * basis[slot_at(slot) + f, t, CORE]
                     )
             return carry
 
         lax.fori_loop(0, RHS, one, 0)
 
     for t in range(2):
-        span = pl.ds(LANES * t, LANES)
-        for k in range(2):
-            stat[k, t, CORE] = cond_ref[k, :, span]
-        for m in range(MONTHS):
-            stat[2 + m, t, CORE] = head_ref[m, :, span]
-        for k in range(2 + MONTHS, 16):
-            stat[k, t, CORE] = jnp.zeros((TILE_ROWS, LANES), F32)
+        stat[15, t, CORE] = jnp.zeros((TILE_ROWS, LANES), F32)
+    sum_in[...] = jnp.zeros_like(sum_in)
+    for load in loads[:5]:
+        load.wait()
+    for t in range(2):
+        stat[ID_FIELD, t, CORE] = id_ref[:, pl.ds(LANES * t, LANES)].astype(F32)
     halo_pack(0, stat, 0, 4)
     pl.semaphore_wait(barrier, group + chips - 2 + len(offsets))
     halo_stat = halo_copies(0, 4, 1)
     for copy in halo_stat:
         copy.start()
 
+    for load in loads[5:]:
+        load.wait()
     scale = (districts / grid_cells) ** 0.5
     ids = id_ref[...]
-    high_id = jnp.zeros_like(ids)
-    for k in range(1, DHI):
-        high_id = high_id + jnp.where(ids >= k * DLO, 1, 0)
-    hi_id[...] = high_id
-    lo_id[...] = ids - DLO * high_id
+    hi_id[pl.ds(0, TILE_ROWS), :] = ids // DLO
+    lo_id[pl.ds(0, TILE_ROWS), :] = lax.rem(ids, DLO)
 
     def hot_line(i, carry):
         same = lo_id[pl.ds(i, 1), :] == rows_of((DLO, 2 * LANES))
-        hot[i] = jnp.where(same, 1.0, 0.0).astype(jnp.bfloat16)
+        hot[:, line_span(i)] = jnp.where(same, 1.0, 0.0).astype(jnp.bfloat16)
         return carry
 
     lax.fori_loop(0, TILE_ROWS, hot_line, 0)
@@ -440,15 +517,16 @@
             square = jnp.zeros((TILE_ROWS, LANES), F32)
             mixed = jnp.zeros((TILE_ROWS, LANES), F32)
             for c in range(CROPS):
-                drawn = wu_ref[m, c] * crops[c]
-                square = square + wu_ref[m, c] * drawn
+                drawn = wu_ref[c, m] * crops[c]
+                square = square + wu_ref[c, m] * drawn
                 mixed = mixed + use_ref[c] * drawn
             diag[m, t] = weight * weight * square + PROXIMAL
             cross[m, t] = weight * live * (scale * mixed)
     for r in range(RHS):
-        for hi in range(DHI):
-            for t in range(3):
-                at = LANES * (3 * hi + t)
+        for t in range(2):
+            bdi[r, t] = jnp.zeros((DHI, LANES), F32)
+            for hi in range(districts // DLO):
+                at = LANES * (2 * hi + t)
                 bdi[r, t, pl.ds(hi, 1)] = rdi_ref[pl.ds(r, 1), pl.ds(at, LANES)]
 
     for copy in halo_stat:
@@ -480,7 +558,7 @@
             diag[m, t] = value
             inverse = 1.0 / value
             dinv[m, t] = inverse
-            crossd[m, t] = cross[m, t] * inverse
+            basis[FIELDS + m, t, CORE] = cross[m, t] * inverse
         return carry
 
     lax.fori_loop(0, MONTHS, month_diag, 0)
@@ -489,38 +567,47 @@
         for t in range(2):
             for m in range(MONTHS):
                 f = r * MONTHS + m
-                basis[f, t, CORE] = rhs_ref[f, :, pl.ds(LANES * t, LANES)] * dinv[m, t]
+                basis[f, t, CORE] = basis[f, t, CORE] * dinv[m, t]
         return carry
 
     lax.fori_loop(0, RHS, start_basis, 0)
 
-    halo_pack(1, basis, 0, FIELDS // 4)
-    halo_first = halo_copies(1, FIELDS // 4, 2)
+    both = (FIELDS + MONTHS) // 4
+    halo_pack(1, basis, 0, both)
+    halo_first = halo_copies(1, both, 2)
     for copy in halo_first:
         copy.start()
     for t in range(2):
         total = jnp.zeros((TILE_ROWS, LANES), F32)
         for m in range(MONTHS):
-            total += cross[m, t] * crossd[m, t]
+            total += cross[m, t] * basis[FIELDS + m, t, CORE]
         cells[1, :, pl.ds(LANES * t, LANES)] = total
     cells_of(core_of(0), 2)
-    sum_in[...] = jnp.zeros_like(sum_in)
     to_district(0, 2 + RHS, 0)
     sum_scatter(0)
 
+    wide_ids()
     for copy in halo_first:
         copy.wait_recv()
-    halo_unpack(1, basis, 0, FIELDS // 4)
+    halo_unpack(1, basis, 0, both)
+    smooth(0, to_second)
     sum_spread(0)
-    smooth(0)
-    cells_of(lambda f, t: image[f, t], 0)
+    halo_pack(2, basis, slot_at(1), FIELDS // 4)
+    halo_second = halo_copies(2, FIELDS // 4, 2)
+    for copy in halo_second:
+        copy.start()
+    cells_of(core_of(1), 0)
     to_district(1, RHS, 0)
     sum_scatter(1)
     sum_gather(0)
+    for copy in halo_second:
+        copy.wait_recv()
+    halo_unpack(2, basis, slot_at(1), FIELDS // 4)
     sum_done(0)
 
     def total_of(n, b):
-        return jnp.stack([sum_out[(n,) + chunk(3 * b + t)] for t in range(3)])
+        parts = [sum_out[(n,) + chunk(4 * b + k)] for k in range(4)]
+        return jnp.stack([jnp.concatenate(parts[:2], axis=0), jnp.concatenate(parts[2:], axis=0)])
 
     diag_di[...] = total_of(0, 0) + PROXIMAL
     wide[...] = total_of(0, 1)
@@ -528,42 +615,36 @@
         t0 = bdi[r] / diag_di[...]
         table[0, r] = t0
         table[1, r] = total_of(0, 2 + r) / diag_di[...] + (1 - SHIFTS[0]) * t0
-    from_district(0, 2, 0)
-    advance(0, 0, SHIFTS[0])
-    halo_pack(2, basis, FIELDS, FIELDS // 4)
-    halo_second = halo_copies(2, FIELDS // 4, 2)
-    for copy in halo_second:
-        copy.start()
     sum_spread(1)
-    for copy in halo_second:
-        copy.wait_recv()
-    halo_unpack(2, basis, FIELDS, FIELDS // 4)
-    smooth(1)
+    from_district(0, 2, 0, LINES)
+    fill_wide_look()
+    advance_wide(SHIFTS[0])
+    sum_gather(1)
+    smooth(1, to_image)
     advance(1, RHS, SHIFTS[1])
-    halo_pack(3, basis, 2 * FIELDS, FIELDS // 4)
+    halo_pack(3, basis, slot_at(2), FIELDS // 4)
     halo_third = halo_copies(3, FIELDS // 4, 2)
     for copy in halo_third:
         copy.start()
-    sum_gather(1)
     cells_of(core_of(2), 0)
     to_district(2, RHS, 0)
-    for copy in halo_third:
-        copy.wait_recv()
-    halo_unpack(3, basis, 2 * FIELDS, FIELDS // 4)
-    smooth(2)
     sum_done(1)
     for r in range(RHS):
         z1 = total_of(1, r) + wide[...] * table[0, r] - SHIFTS[0] * total_of(0, 2 + r)
         table[2, r] = z1 / diag_di[...] + (1 - SHIFTS[1]) * table[1, r]
     from_district(2, 1, 0)
+    for copy in halo_third:
+        copy.wait_recv()
+    halo_unpack(3, basis, slot_at(2), FIELDS // 4)
+    smooth(2, to_image)
     advance(2, 0, SHIFTS[2])
+    halo_pack(4, basis, slot_at(3), FIELDS // 4)
+    halo_fourth = halo_copies(4, FIELDS // 4, 2)
+    for copy in halo_fourth:
+        copy.start()
     cells_of(core_of(3), 0)
     to_district(2, RHS, RHS)
     sum_scatter(2)
-    halo_pack(4, basis, 3 * FIELDS, FIELDS // 4)
-    halo_fourth = halo_copies(4, FIELDS // 4, 2)
-    for copy in halo_fourth:
-        copy.start()
 
     shape = (8, LANES)
 
@@ -571,7 +652,7 @@
         totals = [jnp.zeros(shape, F32) for _ in PAIRS]
         for m in range(MONTHS):
             for t in range(2):
-                values = [basis[s * FIELDS + r * MONTHS + m, t, CORE] for s in range(ITERS)]
+                values = [basis[slot_at(s) + r * MONTHS + m, t, CORE] for s in range(ITERS)]
                 scaled = [diag[m, t] * v for v in values]
                 for n, (i, j) in enumerate(PAIRS):
                     term = scaled[i] * values[j]
@@ -584,16 +665,25 @@
     packed = lax.fori_loop(0, RHS, inner_products, jnp.zeros(shape, F32))
     for copy in halo_fourth:
         copy.wait_recv()
-    halo_unpack(4, basis, 3 * FIELDS, FIELDS // 4)
-    sum_spread(2)
-    smooth(3)
+    halo_unpack(4, basis, slot_at(3), FIELDS // 4)
 
     def top_product(r, packed):
         total = jnp.zeros(shape, F32)
+        base = slot_at(3) + r * MONTHS
+        draws = [[jnp.zeros((TILE_ROWS, LANES), F32)] * CROPS for _ in range(2)]
         for m in range(MONTHS):
+            here = [basis[base + m, t, CORE] for t in range(3)]
+            e, w = beside(here)
             for t in range(2):
-                f = r * MONTHS + m
-                term = diag[m, t] * basis[3 * FIELDS + f, t, CORE] * image[f, t]
+                lap = coefc[4, t] * here[t] - coefc[0, t] * e[t] - coefc[1, t] * w[t]
+                lap = lap - coefc[2, t] * basis[base + m, t, pl.ds(9, 16)]
+                lap = lap - coefc[3, t] * basis[base + m, t, pl.ds(7, 16)]
+                term = stat[2 + m, t, CORE] * lap * lap + PROXIMAL * here[t] * here[t]
+                total = total + (term[:8] + term[8:])
+                draws[t] = [draws[t][c] + wu_ref[c, m] * here[t] for c in range(CROPS)]
+        for t in range(2):
+            for c in range(CROPS):
+                term = wcs[c, t] * draws[t][c] * draws[t][c]
                 total = total + (term[:8] + term[8:])
         here = (rows_of(shape) == r) & (lanes_of(shape) == len(PAIRS))
         return jnp.where(here, jnp.sum(total, keepdims=True), packed)
@@ -613,6 +703,8 @@
 
     lax.fori_loop(1, group, late_first, 0)
     late_near[mine] = late_in[...]
+    sum_spread(2)
+    smooth(3, to_image)
     sum_gather(2)
     bytes_of(late_near.at[pl.ds(1, group - 1)], sum_recv.at[3, 0])
     late_z[chip] = jnp.sum(late_near[...], axis=0)
@@ -695,11 +787,11 @@
         rs = [factors[ITERS + k, pl.ds(r, 1)] for k in range(ITERS + 1)]
         for t in range(2):
             span = pl.ds(LANES * t, LANES)
-            seen = looks[r, :, span]
+            seen = looks[r, pl.ds(0, TILE_ROWS), span]
             for m in range(MONTHS):
                 f = r * MONTHS + m
-                vs = [basis[s * FIELDS + f, t, CORE] for s in range(ITERS)]
-                vs.append(image[f, t] + crossd[m, t] * seen - SHIFTS[3] * vs[3])
+                vs = [basis[slot_at(s) + f, t, CORE] for s in range(ITERS)]
+                vs.append(image[f, t] + basis[FIELDS + m, t, CORE] * seen - SHIFTS[3] * vs[3])
                 dual_ref[f, :, span] = xs[0] * vs[0] + xs[1] * vs[1] + xs[2] * vs[2] + xs[3] * vs[3]
                 total = rs[0] * vs[0]
                 for k in range(1, ITERS + 1):
@@ -711,7 +803,7 @@
     for r in range(RHS):
         xs = [factors[k, pl.ds(r, 1)] for k in range(ITERS)]
         rs = [factors[ITERS + k, pl.ds(r, 1)] for k in range(ITERS + 1)]
-        for t in range(3):
+        for t in range(2):
             dual = xs[0] * table[0, r, t]
             total = rs[0] * table[0, r, t]
             for k in range(1, ITERS):
@@ -719,8 +811,8 @@
             for k in range(1, ITERS + 1):
                 total = total + rs[k] * table[k, r, t]
             total = total * diag_di[t]
-            for hi in range(DHI):
-                span = pl.ds(LANES * (3 * hi + t), LANES)
+            for hi in range(districts // DLO):
+                span = pl.ds(LANES * (2 * hi + t), LANES)
                 dual_di_ref[pl.ds(r, 1), span] = dual[hi : hi + 1]
                 res_di_ref[pl.ds(r, 1), span] = total[hi : hi + 1]
 
@@ -751,7 +843,6 @@
     tile_rows, tile_cols = climate.shape
     grid_cells = tile_rows * rows * tile_cols * cols
     whole = pl.BlockSpec(memory_space=pltpu.VMEM)
-    scalars = pl.BlockSpec(memory_space=pltpu.SMEM)
     block = (FIELDS, tile_rows, tile_cols)
     vmem = lambda *shape: pltpu.VMEM(shape, F32)
     core = (2, TILE_ROWS, LANES)
@@ -763,10 +854,10 @@
             jax.ShapeDtypeStruct(block, F32),
             jax.ShapeDtypeStruct(right_district.shape, F32),
         ),
-        in_specs=[whole] * 8 + [scalars] * 2,
+        in_specs=[pl.BlockSpec(memory_space=pltpu.HBM)] * 10,
         out_specs=(whole,) * 4,
         scratch_shapes=[
-            vmem(ITERS * FIELDS, 3, 32, LANES),
+            vmem(ITERS * FIELDS + MONTHS, 3, 32, LANES),
             vmem(FIELDS, *core),
             vmem(16, 3, 32, LANES),
             vmem(5, 3, 24, LANES),
@@ -775,20 +866,25 @@
             vmem(MONTHS, *core),
             vmem(MONTHS, *core),
             vmem(MONTHS, *core),
-            vmem(MONTHS, *core),
             vmem(CROPS, *core),
             vmem(MONTHS, 3, 24, LANES),
             vmem(CROPS, *core),
-            pltpu.VMEM((TILE_ROWS, DLO, 2 * LANES), jnp.bfloat16),
-            pltpu.VMEM((TILE_ROWS, 2 * LANES), jnp.int32),
-            pltpu.VMEM((TILE_ROWS, 2 * LANES), jnp.int32),
+            pltpu.VMEM((DLO, LINES * 2 * LANES), jnp.bfloat16),
+            pltpu.VMEM((24, 2 * LANES), jnp.int32),
+            pltpu.VMEM((24, 2 * LANES), jnp.int32),
             vmem(2 + RHS, TILE_ROWS, 2 * LANES),
-            vmem(2 * RHS, TILE_ROWS, 2 * LANES),
-            vmem((2 + RHS) * DHI, DLO),
-            vmem(ITERS + 1, RHS, 3, DHI, LANES),
-            vmem(3, DHI, LANES),
-            vmem(3, DHI, LANES),
-            vmem(RHS, 3, DHI, LANES),
+            vmem(2 * RHS, 24, 2 * LANES),
+            vmem(RHS, 3, 32, LANES),
+            pltpu.VMEM((2 * (2 + RHS) * DHI, TILE_ROWS * 2 * LANES), jnp.bfloat16),
+            vmem(*right_district.shape),
+            vmem(*crop_scale.shape),
+            vmem(*climate.shape),
+            pltpu.VMEM(district_id.shape, jnp.int32),
+            pltpu.VMEM(active.shape, jnp.int32),
+            vmem(ITERS + 1, RHS, 2, DHI, LANES),
+            vmem(2, DHI, LANES),
+            vmem(2, DHI, LANES),
+            vmem(RHS, 2, DHI, LANES),
             vmem(3, group, 8 * per, LANES),
             vmem(3, group, 8 * per, LANES),
             vmem(3, chips, 8 * per, LANES),
@@ -797,29 +893,37 @@
             vmem(chips, 8, LANES),
             vmem(8, LANES),
             vmem(2 * ITERS + 1, 8, LANES),
-            vmem(5, 2, FIELDS // 4, 2, 8, LANES),
-            vmem(5, 2, FIELDS // 4, 2, 8, LANES),
+            vmem(5, 2, 15, 2, 8, LANES),
+            vmem(5, 2, 15, 2, 8, LANES),
             vmem(5, 2, TILE_ROWS, LANES),
             vmem(5, 2, 2, 32, LANES),
             pltpu.SemaphoreType.DMA((5, 8)),
             pltpu.SemaphoreType.DMA((5, 8)),
             pltpu.SemaphoreType.DMA((4, 3)),
             pltpu.SemaphoreType.DMA((4, 3)),
+            pltpu.SemaphoreType.DMA((13,)),
+            pltpu.SMEM(water_use.shape[::-1], F32),
+            pltpu.SMEM(district_use.shape, F32),
         ],
         compiler_params=pltpu.CompilerParams(
             collective_id=0, has_side_effects=True, vmem_limit_bytes=48 * 1024 * 1024
         ),
     )(
-        right_aquifer.reshape(block),
-        right_district,
-        head_scale,
-        crop_scale,
-        conductance,
-        climate,
-        district_id,
-        active,
-        water_use,
-        district_use,
+        *(
+            pltpu.with_memory_space_constraint(value, pltpu.HBM)
+            for value in (
+                right_aquifer.reshape(block),
+                right_district,
+                head_scale,
+                crop_scale,
+                conductance,
+                climate,
+                district_id,
+                active,
+                water_use.T,
+                district_use,
+            )
+        )
     )
     dual, dual_di, res, res_di = outs
     return dual.reshape(right_aquifer.shape), dual_di, res.reshape(right_aquifer.shape), res_di

time: 110 us -> 86.5 us (0.79)
  Pallas kernels: 98.7 us -> 82.8 us
  local copies, waits for them, and re-layouts: 10.4 us -> 3 us
    pallas_call x1, Pallas kernels: 98.7 us -> 82.8 us  [body(): pl.pallas_call(functools.partial(kernel, grid_cells), out_shape=(jax.Shap...]
    unnamed x23 -> x4, local copies, waits for them, and re-layouts: 10.4 us -> 3 us
where the time goes in v2:
time: 86.5 us; the launch traced here: 86.4 us
  Pallas kernels  82.8 us (96%)
  local copies, waits for them, and re-layouts  3 us (3%)
    pallas_call x1, Pallas kernels, body(): pl.pallas_call(functools.partial(kernel, grid_cells), out_shape=(jax.Shap...  82.8 us
    unnamed x4, local copies, waits for them, and re-layouts  3 us

profile of v2, /device:TPU:1, one launch (start us, length us, event | category | flops | bytes accessed | tf_op | source)
XLA Modules:
  0.0 86.4 jit_solution(3686846641343252795)
XLA Ops:
  0.6 82.8 %shard_map.129 = (f32[48,16,256]{2,1,0:T(8,128)S(1)}, f32[4,3072]{1,0:T(4,128)S(1)}, f32[48,16,256]{2,1,0:T(8,128)S(1)}, f32[4,3072]{1,0:T(4,128)S(1)}) custom-call(f32[48,16,256]{2,1,0:T(8,128)} %bitcast.6, f32[4,3072]{1,0:T(4,128)} %rdi_hbm.1, f32[12,16,256]{2,1,0:T(8,128)} %head_hbm.1, f32[6,16,256]{2,1,0:T(8,128)} %crop_hbm.1, f32[2,16,256]{2,1,0:T(8,128)} %cond_hbm.1, ...), custom_call_target="tpu_custom_call" | custom-call | tf_op jit(solution)/shard_map/pallas_call | solution.py:849
  83.4 0.9 %copy.18 = f32[4,12,16,256]{3,2,1,0:T(8,128)} copy(f32[4,12,16,256]{3,2,1,0:T(8,128)S(1)} %bitcast.5) | data formatting | bytes 1572864
  84.3 0.6 copy.19
  84.9 0.9 %copy.20 = f32[4,12,16,256]{3,2,1,0:T(8,128)} copy(f32[4,12,16,256]{3,2,1,0:T(8,128)S(1)} %bitcast.4) | data formatting | bytes 1572864
  85.8 0.6 copy.21

commit v3 on v2

--- a/solution.py
+++ b/solution.py
@@ -72,7 +72,6 @@
     cross,
     wcs,
     inner,
-    grads,
     hot,
     lo_id,
     hi_id,
@@ -205,7 +204,7 @@
                     packed = cols_of(32 * g + 4 * k + u, packed, 4 * k + u)
                 return packed
 
-            col_out[n, g] = lax.fori_loop(0, count // 4, quad, jnp.zeros((TILE_ROWS, LANES), F32))
+            col_out[n, g] = lax.fori_loop(0, count // 4, quad, jnp.zeros((TILE_ROWS, LANES), F32), unroll=count // 4)
 
         def rows_quad(k, carry):
             for u in range(4):
@@ -215,7 +214,7 @@
                     row_out[n, 1, k, t, pl.ds(2 * u, 2)] = field[t, pl.ds(8, 2)]
             return carry
 
-        lax.fori_loop(0, quads, rows_quad, 0)
+        lax.fori_loop(0, quads, rows_quad, 0, unroll=quads // 4 if quads % 4 == 0 else 5)
 
     def halo_unpack(n, ref, base, quads):
         shape = (32, LANES)
@@ -233,7 +232,7 @@
                     ref[base + 32 * g + slot, 2] = moved
                 return carry
 
-            lax.fori_loop(0, count // 4, quad, 0)
+            lax.fori_loop(0, count // 4, quad, 0, unroll=count // 4)
 
         def rows_quad(k, carry):
             for u in range(4):
@@ -242,7 +241,7 @@
                     ref[base + 4 * k + u, t, pl.ds(24, 2)] = row_in[n, 1, k, t, pl.ds(2 * u, 2)] * south
             return carry
 
-        lax.fori_loop(0, quads, rows_quad, 0)
+        lax.fori_loop(0, quads, rows_quad, 0, unroll=quads // 4 if quads % 4 == 0 else 5)
 
     def bytes_of(ref, sem):
         pltpu.make_async_copy(ref, ref, sem).wait()
@@ -374,47 +373,57 @@
     def smooth(slot, put):
         def one(r, carry):
             base = slot_at(slot) + r * MONTHS
-            for mb in range(0, MONTHS, 4):
-                months = pl.ds(base + mb, 4)
-                here = [basis[months, t, pl.ds(4, 24)] for t in range(3)]
-                e, w = beside(here)
-                for t in range(3):
-                    n_val = basis[months, t, pl.ds(3, 24)]
-                    s_val = basis[months, t, pl.ds(5, 24)]
-                    lap = coef[4, t] * here[t] - coef[0, t] * e[t] - coef[1, t] * w[t]
-                    lap = lap - coef[2, t] * s_val - coef[3, t] * n_val
-                    inner[pl.ds(mb, 4), t] = headw[pl.ds(mb, 4), t] * lap
-            for t in range(2):
-                totals = [jnp.zeros((TILE_ROWS, LANES), F32)] * CROPS
+            for k in range(3):
+                part, place = pl.ds(8 * k, 8), pl.ds(4 + 8 * k, 8)
+                face = [[coef[j, t, part] for t in range(3)] for j in range(5)]
                 for m in range(MONTHS):
-                    value = basis[base + m, t, CORE]
-                    totals = [totals[c] + wu_ref[c, m] * value for c in range(CROPS)]
-                for c in range(CROPS):
-                    grads[c, t] = totals[c] * wcs[c, t]
-            for mb in range(0, MONTHS, 4):
-                here = [inner[pl.ds(mb, 4), t, pl.ds(4, 16)] for t in range(3)]
-                e, w = beside(here)
-                for t in range(2):
-                    n_val = inner[pl.ds(mb, 4), t, pl.ds(3, 16)]
-                    s_val = inner[pl.ds(mb, 4), t, pl.ds(5, 16)]
-                    lap = coefc[4, t] * here[t] - coefc[0, t] * e[t] - coefc[1, t] * w[t]
-                    lap = lap - coefc[2, t] * s_val - coefc[3, t] * n_val
-                    lap = lap + PROXIMAL * basis[pl.ds(base + mb, 4), t, CORE]
-                    for u in range(4):
-                        m = mb + u
-                        total = lap[u]
+                    here = [basis[base + m, t, place] for t in range(3)]
+                    e, w = beside(here)
+                    for t in range(3):
+                        lap = face[4][t] * here[t] - face[0][t] * e[t] - face[1][t] * w[t]
+                        lap = lap - face[2][t] * basis[base + m, t, pl.ds(5 + 8 * k, 8)]
+                        lap = lap - face[3][t] * basis[base + m, t, pl.ds(3 + 8 * k, 8)]
+                        inner[m, t, part] = headw[m, t, part] * lap
+            for k in range(2):
+                part, place = pl.ds(8 * k, 8), pl.ds(8 + 8 * k, 8)
+                draws = [[jnp.zeros((8, LANES), F32)] * CROPS for _ in range(2)]
+                for m in range(MONTHS):
+                    value = [basis[base + m, t, place] for t in range(2)]
+                    for c in range(CROPS):
+                        for t in range(2):
+                            draws[t][c] = draws[t][c] + wu_ref[c, m] * value[t]
+                draws = [[wcs[c, t, part] * draws[t][c] for c in range(CROPS)] for t in range(2)]
+                face = [[coefc[j, t, part] for t in range(2)] for j in range(5)]
+                for m in range(MONTHS):
+                    here = [inner[m, t, pl.ds(4 + 8 * k, 8)] for t in range(3)]
+                    e, w = beside(here)
+                    for t in range(2):
+                        own = basis[base + m, t, place]
+                        lap = face[4][t] * here[t] - face[0][t] * e[t] - face[1][t] * w[t]
+                        lap = lap - face[2][t] * inner[m, t, pl.ds(5 + 8 * k, 8)]
+                        lap = lap - face[3][t] * inner[m, t, pl.ds(3 + 8 * k, 8)]
+                        total = lap + PROXIMAL * own
                         for c in range(CROPS):
-                            total = total + wu_ref[c, m] * grads[c, t]
-                        put(r * MONTHS + m, t, dinv[m, t] * total)
+                            total = total + wu_ref[c, m] * draws[t][c]
+                        put(r, m, t, k, dinv[m, t, part] * total, own)
             return carry
 
         lax.fori_loop(0, RHS, one, 0)
 
-    def to_image(f, t, value):
-        image[f, t] = value
-
-    def to_second(f, t, value):
-        basis[slot_at(1) + f, t, CORE] = value
+    def to_image(r, m, t, k, value, own):
+        image[r * MONTHS + m, t, pl.ds(8 * k, 8)] = value
+
+    def to_second(r, m, t, k, value, own):
+        basis[slot_at(1) + r * MONTHS + m, t, pl.ds(8 + 8 * k, 8)] = value
+
+    def to_next(slot, look, shift):
+        def put(r, m, t, k, value, own):
+            place = pl.ds(8 + 8 * k, 8)
+            seen = looks[look + r, pl.ds(8 * k, 8), pl.ds(LANES * t, LANES)]
+            value = value + basis[FIELDS + m, t, place] * seen - shift * own
+            basis[slot_at(slot + 1) + r * MONTHS + m, t, place] = value
+
+        return put
 
     def advance_wide(shift):
         window = pl.ds(4, 24)
@@ -463,19 +472,6 @@
             lo_id[pl.ds(16 + k, 1), :] = lax.rem(ids, DLO)
         lax.fori_loop(TILE_ROWS, LINES, hot_line, 0)
 
-    def advance(slot, look, shift):
-        def one(r, carry):
-            for t in range(2):
-                seen = looks[look + r, pl.ds(0, TILE_ROWS), pl.ds(LANES * t, LANES)]
-                for m in range(MONTHS):
-                    f = r * MONTHS + m
-                    basis[slot_at(slot + 1) + f, t, CORE] = (
-                        image[f, t] + basis[FIELDS + m, t, CORE] * seen - shift * basis[slot_at(slot) + f, t, CORE]
-                    )
-            return carry
-
-        lax.fori_loop(0, RHS, one, 0)
-
     for t in range(2):
         stat[15, t, CORE] = jnp.zeros((TILE_ROWS, LANES), F32)
     sum_in[...] = jnp.zeros_like(sum_in)
@@ -484,11 +480,6 @@
     for t in range(2):
         stat[ID_FIELD, t, CORE] = id_ref[:, pl.ds(LANES * t, LANES)].astype(F32)
     halo_pack(0, stat, 0, 4)
-    pl.semaphore_wait(barrier, group + chips - 2 + len(offsets))
-    halo_stat = halo_copies(0, 4, 1)
-    for copy in halo_stat:
-        copy.start()
-
     for load in loads[5:]:
         load.wait()
     scale = (districts / grid_cells) ** 0.5
@@ -529,6 +520,11 @@
                 at = LANES * (2 * hi + t)
                 bdi[r, t, pl.ds(hi, 1)] = rdi_ref[pl.ds(r, 1), pl.ds(at, LANES)]
 
+    pl.semaphore_wait(barrier, group + chips - 2 + len(offsets))
+    halo_stat = halo_copies(0, 4, 1)
+    for copy in halo_stat:
+        copy.start()
+
     for copy in halo_stat:
         copy.wait_recv()
     halo_unpack(0, stat, 0, 4)
@@ -587,22 +583,19 @@
     sum_scatter(0)
 
     wide_ids()
+    sum_spread(0)
     for copy in halo_first:
         copy.wait_recv()
     halo_unpack(1, basis, 0, both)
     smooth(0, to_second)
-    sum_spread(0)
     halo_pack(2, basis, slot_at(1), FIELDS // 4)
     halo_second = halo_copies(2, FIELDS // 4, 2)
     for copy in halo_second:
         copy.start()
+    sum_gather(0)
     cells_of(core_of(1), 0)
     to_district(1, RHS, 0)
     sum_scatter(1)
-    sum_gather(0)
-    for copy in halo_second:
-        copy.wait_recv()
-    halo_unpack(2, basis, slot_at(1), FIELDS // 4)
     sum_done(0)
 
     def total_of(n, b):
@@ -615,17 +608,19 @@
         t0 = bdi[r] / diag_di[...]
         table[0, r] = t0
         table[1, r] = total_of(0, 2 + r) / diag_di[...] + (1 - SHIFTS[0]) * t0
-    sum_spread(1)
     from_district(0, 2, 0, LINES)
     fill_wide_look()
+    for copy in halo_second:
+        copy.wait_recv()
+    halo_unpack(2, basis, slot_at(1), FIELDS // 4)
+    sum_spread(1)
     advance_wide(SHIFTS[0])
-    sum_gather(1)
-    smooth(1, to_image)
-    advance(1, RHS, SHIFTS[1])
+    smooth(1, to_next(1, RHS, SHIFTS[1]))
     halo_pack(3, basis, slot_at(2), FIELDS // 4)
     halo_third = halo_copies(3, FIELDS // 4, 2)
     for copy in halo_third:
         copy.start()
+    sum_gather(1)
     cells_of(core_of(2), 0)
     to_district(2, RHS, 0)
     sum_done(1)
@@ -636,8 +631,7 @@
     for copy in halo_third:
         copy.wait_recv()
     halo_unpack(3, basis, slot_at(2), FIELDS // 4)
-    smooth(2, to_image)
-    advance(2, 0, SHIFTS[2])
+    smooth(2, to_next(2, 0, SHIFTS[2]))
     halo_pack(4, basis, slot_at(3), FIELDS // 4)
     halo_fourth = halo_copies(4, FIELDS // 4, 2)
     for copy in halo_fourth:
@@ -663,6 +657,7 @@
         return packed
 
     packed = lax.fori_loop(0, RHS, inner_products, jnp.zeros(shape, F32))
+    sum_spread(2)
     for copy in halo_fourth:
         copy.wait_recv()
     halo_unpack(4, basis, slot_at(3), FIELDS // 4)
@@ -703,7 +698,6 @@
 
     lax.fori_loop(1, group, late_first, 0)
     late_near[mine] = late_in[...]
-    sum_spread(2)
     smooth(3, to_image)
     sum_gather(2)
     bytes_of(late_near.at[pl.ds(1, group - 1)], sum_recv.at[3, 0])
@@ -868,7 +862,6 @@
             vmem(MONTHS, *core),
             vmem(CROPS, *core),
             vmem(MONTHS, 3, 24, LANES),
-            vmem(CROPS, *core),
             pltpu.VMEM((DLO, LINES * 2 * LANES), jnp.bfloat16),
             pltpu.VMEM((24, 2 * LANES), jnp.int32),
             pltpu.VMEM((24, 2 * LANES), jnp.int32),

time: 86.5 us -> 78.8 us (0.911)
  Pallas kernels: 82.8 us -> 75.1 us
    pallas_call x1, Pallas kernels: 82.8 us -> 75.1 us  [body(): pl.pallas_call(functools.partial(kernel, grid_cells), out_shape=(jax.Shap...]
where the time goes in v3:
time: 78.8 us; the launch traced here: 78.7 us
  Pallas kernels  75.1 us (95%)
  local copies, waits for them, and re-layouts  3 us (4%)
    pallas_call x1, Pallas kernels, body(): pl.pallas_call(functools.partial(kernel, grid_cells), out_shape=(jax.Shap...  75.1 us
    unnamed x4, local copies, waits for them, and re-layouts  3 us

profile of v3, /device:TPU:1, one launch (start us, length us, event | category | flops | bytes accessed | tf_op | source)
XLA Modules:
  0.0 78.7 jit_solution(2606056106012823623)
XLA Ops:
  0.6 75.1 %shard_map.129 = (f32[48,16,256]{2,1,0:T(8,128)S(1)}, f32[4,3072]{1,0:T(4,128)S(1)}, f32[48,16,256]{2,1,0:T(8,128)S(1)}, f32[4,3072]{1,0:T(4,128)S(1)}) custom-call(f32[48,16,256]{2,1,0:T(8,128)} %bitcast.6, f32[4,3072]{1,0:T(4,128)} %rdi_hbm.1, f32[12,16,256]{2,1,0:T(8,128)} %head_hbm.1, f32[6,16,256]{2,1,0:T(8,128)} %crop_hbm.1, f32[2,16,256]{2,1,0:T(8,128)} %cond_hbm.1, ...), custom_call_target="tpu_custom_call" | custom-call | tf_op jit(solution)/shard_map/pallas_call | solution.py:843
  75.7 0.9 %copy.18 = f32[4,12,16,256]{3,2,1,0:T(8,128)} copy(f32[4,12,16,256]{3,2,1,0:T(8,128)S(1)} %bitcast.5) | data formatting | bytes 1572864
  76.6 0.6 copy.19
  77.2 0.9 %copy.20 = f32[4,12,16,256]{3,2,1,0:T(8,128)} copy(f32[4,12,16,256]{3,2,1,0:T(8,128)S(1)} %bitcast.4) | data formatting | bytes 1572864
  78.1 0.6 copy.21

commit v4 on v3

--- a/solution.py
+++ b/solution.py
@@ -17,7 +17,7 @@
 LANES = 128
 TILE_ROWS = 16
 CHUNKS = 32
-LINES = 21
+LINES = 22
 ID_FIELD = 14
 PROXIMAL = 0.05
 SHIFTS = (0.5, 8.0, 3.0, 1.0)
@@ -188,7 +188,7 @@
             for k, (src, dst, to) in enumerate(plan)
         ]
 
-    def halo_pack(n, ref, base, quads):
+    def halo_pack_cols(n, ref, base, quads):
         lane = lanes_of((TILE_ROWS, LANES))
 
         def cols_of(f, packed, slot):
@@ -206,6 +206,7 @@
 
             col_out[n, g] = lax.fori_loop(0, count // 4, quad, jnp.zeros((TILE_ROWS, LANES), F32), unroll=count // 4)
 
+    def halo_pack_rows(n, ref, base, quads):
         def rows_quad(k, carry):
             for u in range(4):
                 field = ref.at[base + 4 * k + u]
@@ -216,7 +217,26 @@
 
         lax.fori_loop(0, quads, rows_quad, 0, unroll=quads // 4 if quads % 4 == 0 else 5)
 
-    def halo_unpack(n, ref, base, quads):
+    def send_cols(n, ref, base, quads):
+        copies = halo_copies(n, quads, (quads + 7) // 8)
+        halo_pack_cols(n, ref, base, quads)
+        for copy in copies[2:]:
+            copy.start()
+        return copies
+
+    def send_rows(copies, n, ref, base, quads):
+        halo_pack_rows(n, ref, base, quads)
+        for copy in copies[:2]:
+            copy.start()
+
+    def halo_send(n, ref, base, quads):
+        copies = send_cols(n, ref, base, quads)
+        send_rows(copies, n, ref, base, quads)
+        return copies
+
+    def halo_cols(copies, n, ref, base, quads):
+        for copy in copies[2:]:
+            copy.wait_recv()
         shape = (32, LANES)
         lane, place = lanes_of(shape), rows_of(shape)
         side = jnp.where(lax.rem(lane, 4) < 2, west, east)
@@ -233,6 +253,10 @@
                 return carry
 
             lax.fori_loop(0, count // 4, quad, 0, unroll=count // 4)
+
+    def halo_rows(copies, n, ref, base, quads):
+        for copy in copies[:2]:
+            copy.wait_recv()
 
         def rows_quad(k, carry):
             for u in range(4):
@@ -346,15 +370,17 @@
         high = values.astype(jnp.bfloat16).astype(F32)
         both = jnp.concatenate([high, values - high], axis=0).astype(jnp.bfloat16)
 
-        def line(i, carry):
-            picked = jnp.dot(both, hot[:, line_span(i)], preferred_element_type=F32)
-            picked = (picked[:size] + picked[size:]).reshape(count * RHS, DHI, 2 * LANES)
-            here = (hi_id[pl.ds(i, 1), :] == rows_of((DHI, 2 * LANES)))[None]
-            picked = jnp.where(here, picked, 0.0)
-            looks[pl.ds(first, count * RHS), pl.ds(i, 1), :] = jnp.sum(picked, axis=1, keepdims=True)
+        def two(k, carry):
+            span = pl.ds(pl.multiple_of(k * (4 * LANES), 4 * LANES), 4 * LANES)
+            picked = jnp.dot(both, hot[:, span], preferred_element_type=F32)
+            picked = (picked[:size] + picked[size:]).reshape(count * RHS, DHI, 4 * LANES)
+            for u in range(2):
+                here = (hi_id[pl.ds(2 * k + u, 1), :] == rows_of((DHI, 2 * LANES)))[None]
+                part = jnp.where(here, picked[:, :, 2 * LANES * u : 2 * LANES * (u + 1)], 0.0)
+                looks[pl.ds(first, count * RHS), pl.ds(2 * k + u, 1), :] = jnp.sum(part, axis=1, keepdims=True)
             return carry
 
-        lax.fori_loop(0, lines, line, 0, unroll=3 if lines % 3 == 0 else 2)
+        lax.fori_loop(0, lines // 2, two, 0, unroll=lines // 2 if count == 1 else 1)
 
     def cells_of(load, first):
         def one(r, carry):
@@ -470,7 +496,7 @@
             ids = one.astype(jnp.int32)
             hi_id[pl.ds(16 + k, 1), :] = ids // DLO
             lo_id[pl.ds(16 + k, 1), :] = lax.rem(ids, DLO)
-        lax.fori_loop(TILE_ROWS, LINES, hot_line, 0)
+        lax.fori_loop(TILE_ROWS, LINES - 1, hot_line, 0)
 
     for t in range(2):
         stat[15, t, CORE] = jnp.zeros((TILE_ROWS, LANES), F32)
@@ -479,7 +505,8 @@
         load.wait()
     for t in range(2):
         stat[ID_FIELD, t, CORE] = id_ref[:, pl.ds(LANES * t, LANES)].astype(F32)
-    halo_pack(0, stat, 0, 4)
+    halo_pack_cols(0, stat, 0, 4)
+    halo_pack_rows(0, stat, 0, 4)
     for load in loads[5:]:
         load.wait()
     scale = (districts / grid_cells) ** 0.5
@@ -525,9 +552,8 @@
     for copy in halo_stat:
         copy.start()
 
-    for copy in halo_stat:
-        copy.wait_recv()
-    halo_unpack(0, stat, 0, 4)
+    halo_rows(halo_stat, 0, stat, 0, 4)
+    halo_cols(halo_stat, 0, stat, 0, 4)
     window = pl.ds(4, 24)
     faces = [[stat[k, t, window] for t in range(3)] for k in range(2)]
     east_side, west_side = beside(faces[0])
@@ -557,7 +583,7 @@
             basis[FIELDS + m, t, CORE] = cross[m, t] * inverse
         return carry
 
-    lax.fori_loop(0, MONTHS, month_diag, 0)
+    lax.fori_loop(0, MONTHS, month_diag, 0, unroll=4)
 
     def start_basis(r, carry):
         for t in range(2):
@@ -569,10 +595,7 @@
     lax.fori_loop(0, RHS, start_basis, 0)
 
     both = (FIELDS + MONTHS) // 4
-    halo_pack(1, basis, 0, both)
-    halo_first = halo_copies(1, both, 2)
-    for copy in halo_first:
-        copy.start()
+    halo_first = halo_send(1, basis, 0, both)
     for t in range(2):
         total = jnp.zeros((TILE_ROWS, LANES), F32)
         for m in range(MONTHS):
@@ -584,18 +607,15 @@
 
     wide_ids()
     sum_spread(0)
-    for copy in halo_first:
-        copy.wait_recv()
-    halo_unpack(1, basis, 0, both)
+    halo_rows(halo_first, 1, basis, 0, both)
+    halo_cols(halo_first, 1, basis, 0, both)
     smooth(0, to_second)
-    halo_pack(2, basis, slot_at(1), FIELDS // 4)
-    halo_second = halo_copies(2, FIELDS // 4, 2)
-    for copy in halo_second:
-        copy.start()
+    halo_second = halo_send(2, basis, slot_at(1), FIELDS // 4)
     sum_gather(0)
     cells_of(core_of(1), 0)
     to_district(1, RHS, 0)
     sum_scatter(1)
+    halo_rows(halo_second, 2, basis, slot_at(1), FIELDS // 4)
     sum_done(0)
 
     def total_of(n, b):
@@ -610,16 +630,11 @@
         table[1, r] = total_of(0, 2 + r) / diag_di[...] + (1 - SHIFTS[0]) * t0
     from_district(0, 2, 0, LINES)
     fill_wide_look()
-    for copy in halo_second:
-        copy.wait_recv()
-    halo_unpack(2, basis, slot_at(1), FIELDS // 4)
+    halo_cols(halo_second, 2, basis, slot_at(1), FIELDS // 4)
     sum_spread(1)
     advance_wide(SHIFTS[0])
     smooth(1, to_next(1, RHS, SHIFTS[1]))
-    halo_pack(3, basis, slot_at(2), FIELDS // 4)
-    halo_third = halo_copies(3, FIELDS // 4, 2)
-    for copy in halo_third:
-        copy.start()
+    halo_third = halo_send(3, basis, slot_at(2), FIELDS // 4)
     sum_gather(1)
     cells_of(core_of(2), 0)
     to_district(2, RHS, 0)
@@ -628,17 +643,14 @@
         z1 = total_of(1, r) + wide[...] * table[0, r] - SHIFTS[0] * total_of(0, 2 + r)
         table[2, r] = z1 / diag_di[...] + (1 - SHIFTS[1]) * table[1, r]
     from_district(2, 1, 0)
-    for copy in halo_third:
-        copy.wait_recv()
-    halo_unpack(3, basis, slot_at(2), FIELDS // 4)
+    halo_rows(halo_third, 3, basis, slot_at(2), FIELDS // 4)
+    halo_cols(halo_third, 3, basis, slot_at(2), FIELDS // 4)
     smooth(2, to_next(2, 0, SHIFTS[2]))
-    halo_pack(4, basis, slot_at(3), FIELDS // 4)
-    halo_fourth = halo_copies(4, FIELDS // 4, 2)
-    for copy in halo_fourth:
-        copy.start()
+    halo_fourth = send_cols(4, basis, slot_at(3), FIELDS // 4)
     cells_of(core_of(3), 0)
     to_district(2, RHS, RHS)
     sum_scatter(2)
+    send_rows(halo_fourth, 4, basis, slot_at(3), FIELDS // 4)
 
     shape = (8, LANES)
 
@@ -658,9 +670,8 @@
 
     packed = lax.fori_loop(0, RHS, inner_products, jnp.zeros(shape, F32))
     sum_spread(2)
-    for copy in halo_fourth:
-        copy.wait_recv()
-    halo_unpack(4, basis, slot_at(3), FIELDS // 4)
+    halo_rows(halo_fourth, 4, basis, slot_at(3), FIELDS // 4)
+    halo_cols(halo_fourth, 4, basis, slot_at(3), FIELDS // 4)
 
     def top_product(r, packed):
         total = jnp.zeros(shape, F32)
@@ -683,7 +694,7 @@
         here = (rows_of(shape) == r) & (lanes_of(shape) == len(PAIRS))
         return jnp.where(here, jnp.sum(total, keepdims=True), packed)
 
-    late_in[...] = lax.fori_loop(0, RHS, top_product, packed)
+    late_in[...] = lax.fori_loop(0, RHS, top_product, packed, unroll=2)
 
     def late_first(k, carry):
         pltpu.make_async_remote_copy(
@@ -715,12 +726,6 @@
         return carry
 
     lax.fori_loop(1, chips, late_second, 0)
-    sum_done(2)
-    for r in range(RHS):
-        table[3, r] = total_of(2, r) / diag_di[...] + (1 - SHIFTS[2]) * table[2, r]
-        table[4, r] = total_of(2, RHS + r) / diag_di[...] + (1 - SHIFTS[3]) * table[3, r]
-    from_district(3, 1, 0)
-
     def district_part(i, j):
         out = jnp.zeros(shape, F32)
         for r in range(RHS):
@@ -732,7 +737,14 @@
             out = jnp.where(rows_of(shape) == r, line, out)
         return out
 
-    parts = [district_part(i, j) for i, j in PAIRS + ((3, ITERS),)]
+    early = {pair: district_part(*pair) for pair in PAIRS if pair[1] < 3}
+    sum_done(2)
+    for r in range(RHS):
+        table[3, r] = total_of(2, r) / diag_di[...] + (1 - SHIFTS[2]) * table[2, r]
+        table[4, r] = total_of(2, RHS + r) / diag_di[...] + (1 - SHIFTS[3]) * table[3, r]
+    from_district(3, 1, 0)
+
+    parts = [early[pair] if pair in early else district_part(*pair) for pair in PAIRS + ((3, ITERS),)]
     bytes_of(late_z.at[pl.ds(1, chips - 1)], sum_recv.at[3, 1])
     totals = jnp.sum(late_z[...], axis=0)
     gram = [[None] * (ITERS + 1) for _ in range(ITERS + 1)]

time: 78.8 us -> 76.4 us (0.970)
  Pallas kernels: 75.1 us -> 72.7 us
    pallas_call x1, Pallas kernels: 75.1 us -> 72.7 us  [body(): pl.pallas_call(functools.partial(kernel, grid_cells), out_shape=(jax.Shap...]
where the time goes in v4:
time: 76.4 us; the launch traced here: 76.3 us
  Pallas kernels  72.7 us (95%)
  local copies, waits for them, and re-layouts  3 us (4%)
    pallas_call x1, Pallas kernels, body(): pl.pallas_call(functools.partial(kernel, grid_cells), out_shape=(jax.Shap...  72.7 us
    unnamed x4, local copies, waits for them, and re-layouts  3 us

profile of v4, /device:TPU:1, one launch (start us, length us, event | category | flops | bytes accessed | tf_op | source)
XLA Modules:
  0.0 76.3 jit_solution(11156148281135502588)
XLA Ops:
  0.6 72.7 %shard_map.129 = (f32[48,16,256]{2,1,0:T(8,128)S(1)}, f32[4,3072]{1,0:T(4,128)S(1)}, f32[48,16,256]{2,1,0:T(8,128)S(1)}, f32[4,3072]{1,0:T(4,128)S(1)}) custom-call(f32[48,16,256]{2,1,0:T(8,128)} %bitcast.6, f32[4,3072]{1,0:T(4,128)} %rdi_hbm.1, f32[12,16,256]{2,1,0:T(8,128)} %head_hbm.1, f32[6,16,256]{2,1,0:T(8,128)} %crop_hbm.1, f32[2,16,256]{2,1,0:T(8,128)} %cond_hbm.1, ...), custom_call_target="tpu_custom_call" | custom-call | tf_op jit(solution)/shard_map/pallas_call | solution.py:855
  73.3 0.9 %copy.18 = f32[4,12,16,256]{3,2,1,0:T(8,128)} copy(f32[4,12,16,256]{3,2,1,0:T(8,128)S(1)} %bitcast.5) | data formatting | bytes 1572864
  74.2 0.6 copy.19
  74.8 0.9 %copy.20 = f32[4,12,16,256]{3,2,1,0:T(8,128)} copy(f32[4,12,16,256]{3,2,1,0:T(8,128)S(1)} %bitcast.4) | data formatting | bytes 1572864
  75.7 0.6 copy.21

commit v5 on v4

--- a/solution.py
+++ b/solution.py
@@ -638,12 +638,12 @@
     sum_gather(1)
     cells_of(core_of(2), 0)
     to_district(2, RHS, 0)
+    halo_rows(halo_third, 3, basis, slot_at(2), FIELDS // 4)
     sum_done(1)
     for r in range(RHS):
         z1 = total_of(1, r) + wide[...] * table[0, r] - SHIFTS[0] * total_of(0, 2 + r)
         table[2, r] = z1 / diag_di[...] + (1 - SHIFTS[1]) * table[1, r]
     from_district(2, 1, 0)
-    halo_rows(halo_third, 3, basis, slot_at(2), FIELDS // 4)
     halo_cols(halo_third, 3, basis, slot_at(2), FIELDS // 4)
     smooth(2, to_next(2, 0, SHIFTS[2]))
     halo_fourth = send_cols(4, basis, slot_at(3), FIELDS // 4)

time: 76.4 us -> 76.3 us (level)
  no operation moved by 1% of the time
where the time goes in v5:
time: 76.3 us; the launch traced here: 76.2 us
  Pallas kernels  72.6 us (95%)
  local copies, waits for them, and re-layouts  3 us (4%)
    pallas_call x1, Pallas kernels, body(): pl.pallas_call(functools.partial(kernel, grid_cells), out_shape=(jax.Shap...  72.6 us
    unnamed x4, local copies, waits for them, and re-layouts  3 us

profile of v5, /device:TPU:1, one launch (start us, length us, event | category | flops | bytes accessed | tf_op | source)
XLA Modules:
  0.0 76.2 jit_solution(17617323049589280020)
XLA Ops:
  0.6 72.6 %shard_map.129 = (f32[48,16,256]{2,1,0:T(8,128)S(1)}, f32[4,3072]{1,0:T(4,128)S(1)}, f32[48,16,256]{2,1,0:T(8,128)S(1)}, f32[4,3072]{1,0:T(4,128)S(1)}) custom-call(f32[48,16,256]{2,1,0:T(8,128)} %bitcast.6, f32[4,3072]{1,0:T(4,128)} %rdi_hbm.1, f32[12,16,256]{2,1,0:T(8,128)} %head_hbm.1, f32[6,16,256]{2,1,0:T(8,128)} %crop_hbm.1, f32[2,16,256]{2,1,0:T(8,128)} %cond_hbm.1, ...), custom_call_target="tpu_custom_call" | custom-call | tf_op jit(solution)/shard_map/pallas_call | solution.py:855
  73.2 0.9 %copy.18 = f32[4,12,16,256]{3,2,1,0:T(8,128)} copy(f32[4,12,16,256]{3,2,1,0:T(8,128)S(1)} %bitcast.5) | data formatting | bytes 1572864
  74.1 0.6 copy.19
  74.7 0.9 %copy.20 = f32[4,12,16,256]{3,2,1,0:T(8,128)} copy(f32[4,12,16,256]{3,2,1,0:T(8,128)S(1)} %bitcast.4) | data formatting | bytes 1572864
  75.6 0.6 copy.21
